TPU v7x, 32 devices: a whole 2x2x4 slice. The times are simulated.
32 devices in a mesh: groups: 2 (over y), head: 4 (over z), req: 2 (over x), seq: 2 (over core).
Axes of the slice: x: 2, y: 2, z: 4, core: 2. Of those that a mesh axis runs over, the one named last changes fastest.
Arguments:
- queries: bfloat16 [4, 256, 6144], P(('groups', 'req'), 'seq', 'head'), parts along dimension 0, may hold values from -400 to 400
- hidden: bfloat16 [4, 256, 7168], P(('groups', 'req'), 'seq', 'head'), parts along dimension 0, may hold values from -6 to 6
- w_dkv: bfloat16 [7168, 576], P('head'), may hold values from -0.0625 to 0.0625
- kv_gain: float32 [512], replicated, may hold values from 0.1 to 1.9
- w_uk: bfloat16 [32, 128, 512], P('head'), may hold values from -0.5 to 0.5
- value_up_weight: bfloat16 [32, 512, 128], P('head'), may hold values from -0.25 to 0.25
- page_pool: bfloat16 [512, 36864], P(('groups', 'head', 'req')), parts along dimension 0, may hold values from -6 to 6
- page_owner: int32 [4, 64, 1], P('groups'), parts along dimension 0, may hold values from 0 to 7; in each aligned block of 64 rows (0 to 63, 64 to 127, ..., all dimensions but the last counted through in order) at most 16 rows name the same one
- page_slot: int32 [4, 64], P('groups'), parts along dimension 0, may hold values from 0 to 31
- prefix_len: int32 [4], P('groups'), parts along dimension 0, may hold values from 64 to 4096, as said below
- suffix_len: int32 [4], P('groups'), parts along dimension 0, may hold values from 128 to 256, as said below
Outputs:
- attn_out: bfloat16 [4, 256, 4096], P(('groups', 'req'), 'seq', 'head'), parts along dimension 0
- new_pages: bfloat16 [4, 4, 36864], P(('groups', 'req'), 'seq'), parts along dimension 0
There are 2 independent parts, one for each index of `groups`. A program takes and returns all parts, laid end to end along the dimension named above; an argument that names none is the same for every part. Nothing has to cross between parts.
Inputs may be any that keep to these rules, and one draw needn't show every extreme that they name: `page_owner`: in the rows of one request batch (1 request) no owner holds more than 16 pages, and some owner holds exactly 16. `prefix_len`: some request has the longest prefix. `suffix_len`: some request fills all suffix slots.
All inputs are finite; a program needn't handle non-finite values.
Results may differ from a plain program's by a relative error of at most 0.0055.
The roundings to bfloat16 on the way count: a program that leaves them out, or rounds other values in their place, can miss the bound.
Values may be sent and summed in bfloat16 or wider, within the bound.
No kernel may reach another device: no remote copies, remote signals or barrier semaphores. Data moves between devices by JAX's collectives and lax.ppermute only.
A program may use at most 128 MiB of HBM per device.

v0:
```python
import jax
import jax.numpy as jnp
from jax import lax
from jax.sharding import PartitionSpec as P


def from_behind(block, axis, distance):
    devices = range(lax.axis_size(axis))
    route = [(i - distance, i) for i in devices if i - distance in devices]
    return lax.ppermute(block, axis, route)


def rotate(vector, cosine_table, sine_table):
    half_width = vector.shape[-1] // 2
    first_half = vector[..., :half_width]
    second_half = vector[..., half_width:]
    return jnp.concatenate(
        [
            first_half * cosine_table - second_half * sine_table,
            first_half * sine_table + second_half * cosine_table,
        ],
        axis=-1,
    )


def angles(positions, rope_width):
    half_width = rope_width // 2
    frequency = 10000.0 ** (-2.0 * jnp.arange(half_width, dtype=jnp.float32) / rope_width)
    phases = positions.astype(jnp.float32)[:, None] * frequency[None, :]
    return (jnp.cos(phases), jnp.sin(phases))


def finish_latent(summed, positions, live_rows, kv_gain, latent_width):
    latent_part = summed[:, :latent_width]
    mean_square = jnp.mean(latent_part * latent_part, axis=-1, keepdims=True)
    normed = latent_part * lax.rsqrt(mean_square + 1e-06) * kv_gain
    cosine_table, sine_table = angles(positions, summed.shape[1] - latent_width)
    rotated = rotate(summed[:, latent_width:], cosine_table, sine_table)
    joined = jnp.concatenate([normed, rotated], axis=-1).astype(jnp.bfloat16)
    return jnp.where(live_rows[:, None], joined, jnp.zeros_like(joined))


def local(
    queries,
    hidden,
    w_dkv,
    kv_gain,
    w_uk,
    value_up_weight,
    page_pool,
    page_owner,
    page_slot,
    prefix_len,
    suffix_len,
):
    n_head = lax.axis_size("head")
    n_req = lax.axis_size("req")
    head_idx = lax.axis_index("head")
    req_idx = lax.axis_index("req")
    seq_idx = lax.axis_index("seq")
    req_dev, half_len, d_local = hidden.shape
    heads_dev, nope_width, latent_width = w_uk.shape
    value_width = value_up_weight.shape[2]
    lat_width = w_dkv.shape[1]
    rope_width = lat_width - latent_width
    query_width = queries.shape[2] // heads_dev
    page_width = page_pool.shape[1]
    page_len = page_width // lat_width
    pages_req = page_slot.shape[1]
    batch_rows = req_dev * pages_req
    owners = n_head * n_req
    slot_cap = max(2, 2 * batch_rows // owners)
    score_scale = float(query_width) ** (-0.5)
    my_prefix = lax.dynamic_slice_in_dim(prefix_len, req_idx * req_dev, req_dev)
    my_suffix = lax.dynamic_slice_in_dim(suffix_len, req_idx * req_dev, req_dev)
    local_t = jnp.arange(half_len, dtype=jnp.int32)
    glob_t = seq_idx * half_len + local_t
    positions = my_prefix[:, None] + glob_t[None, :]
    live_rows = glob_t[None, :] < my_suffix[:, None]
    partial_value = jnp.dot(
        hidden.reshape(req_dev * half_len, d_local), w_dkv, preferred_element_type=jnp.float32
    )
    summed = lax.psum(partial_value, "head")
    new_flat = finish_latent(
        summed, positions.reshape(-1), live_rows.reshape(-1), kv_gain, latent_width
    )
    fresh_latent = new_flat.reshape(req_dev, half_len, lat_width)
    new_pages = fresh_latent.reshape(req_dev, half_len // page_len, page_len * lat_width)
    earlier = from_behind(fresh_latent, "seq", 1)
    owner_rows = page_owner[:, :, 0]
    row_order = jnp.arange(batch_rows, dtype=jnp.int32)
    before = row_order[None, :] < row_order[:, None]
    same_owner = owner_rows[:, :, None] == owner_rows[:, None, :]
    owner_rank = jnp.sum((same_owner & before[None]).astype(jnp.int32), axis=2)
    self_owner = head_idx * n_req + req_idx
    slot_ids = jnp.arange(slot_cap, dtype=jnp.int32)
    picked = (owner_rows == self_owner)[:, None, :] & (
        owner_rank[:, None, :] == slot_ids[None, :, None]
    )
    chosen = jnp.sum(jnp.where(picked, page_slot[:, None, :], 0), axis=2)
    present = jnp.any(picked, axis=2)
    outgoing = jnp.where(present[:, :, None], page_pool[chosen], jnp.zeros((), page_pool.dtype))
    arrived = lax.all_to_all(outgoing, "req", split_axis=0, concat_axis=0, tiled=True)
    received = lax.all_gather(arrived, "head", axis=0, tiled=True)
    own_owner = lax.dynamic_index_in_dim(owner_rows, req_idx, 0, keepdims=False)
    own_rank = lax.dynamic_index_in_dim(owner_rank, req_idx, 0, keepdims=False)
    cached = received.reshape(owners * slot_cap, page_width)[own_owner * slot_cap + own_rank]
    prefix_width = pages_req * page_len
    cached = cached.reshape(req_dev, prefix_width, lat_width)
    key_places = jnp.arange(prefix_width, dtype=jnp.int32)
    suffix_places = jnp.concatenate([(seq_idx - 1) * half_len + local_t, glob_t], axis=0)
    key_latent = jnp.concatenate([cached[0], earlier[0], fresh_latent[0]], axis=0)
    query_rows = queries[0].reshape(half_len, heads_dev, query_width)
    q_latent = jnp.einsum(
        "thn,hnk->thk", query_rows[..., :nope_width], w_uk, preferred_element_type=jnp.float32
    ).astype(jnp.bfloat16)
    cosine_table, sine_table = angles(positions[0], rope_width)
    q_rotated = rotate(
        query_rows[..., nope_width:].astype(jnp.float32),
        cosine_table[:, None, :],
        sine_table[:, None, :],
    ).astype(jnp.bfloat16)
    q_full = jnp.concatenate([q_latent, q_rotated], axis=-1)
    scores = (
        jnp.einsum("thk,jk->htj", q_full, key_latent, preferred_element_type=jnp.float32)
        * score_scale
    )
    far_allowed = jnp.broadcast_to(key_places[None, :] < my_prefix[0], (half_len, prefix_width))
    near_allowed = (
        (suffix_places[None, :] >= 0)
        & (suffix_places[None, :] <= glob_t[:, None])
        & (suffix_places[None, :] < my_suffix[0])
    )
    allowed = jnp.concatenate([far_allowed, near_allowed], axis=1)
    scores = jnp.where(allowed[None], scores, -jnp.inf)
    row_max = jnp.max(scores, axis=-1, keepdims=True)
    exponent = jnp.exp(scores - row_max)
    weights = (exponent / jnp.sum(exponent, axis=-1, keepdims=True)).astype(jnp.bfloat16)
    output_latent = jnp.einsum(
        "htj,jk->thk", weights, key_latent[:, :latent_width], preferred_element_type=jnp.float32
    ).astype(jnp.bfloat16)
    per_head_output = jnp.einsum(
        "wsd,sdp->wsp", output_latent, value_up_weight, preferred_element_type=jnp.float32
    ).reshape(half_len, heads_dev * value_width)
    outputs = [
        jnp.where(live_rows[0][:, None], per_head_output, jnp.zeros_like(per_head_output)).astype(
            jnp.bfloat16
        )
    ]
    attn_out = jnp.stack(outputs, axis=0)
    return (attn_out, new_pages)


def solution(mesh):
    placed = (
        P(("groups", "req"), "seq", "head"),
        P(("groups", "req"), "seq", "head"),
        P("head", None),
        P(),
        P("head", None, None),
        P("head", None, None),
        P(("groups", "head", "req"), None),
        P("groups", None, None),
        P("groups", None),
        P("groups"),
        P("groups"),
    )
    return jax.shard_map(
        local,
        mesh=mesh,
        in_specs=placed,
        out_specs=(P(("groups", "req"), "seq", "head"), P(("groups", "req"), "seq", None)),
        check_vma=False,
    )
```

profile of v0, /device:TPU:0, one launch (start us, length us, event | category | flops | bytes accessed | tf_op | source)
XLA Modules:
  0.0 323.1 jit_solution(2699671156256365024)
XLA Ops:
  7.2 0.0 copy-start
  7.2 0.8 broadcast_compare_fusion.2
  8.0 0.9 convert_reduce_fusion
  9.0 0.1 fusion.20
  9.1 0.8 select_reduce_fusion
  9.9 0.1 reshape.332
  10.0 0.0 copy-done
  10.0 3.5 %gather_fusion = bf16[32,36864]{1,0:T(8,128)(2,1)} fusion(bf16[32,36864]{1,0:T(8,128)(2,1)S(1)} %copy-done, s32[1024]{0:T(1024)S(1)} %pad_clamp_fusion.1), kind=kCustom, calls=%fused_computation | custom fusion | bytes 4718720 | tf_op jit(solution)/shard_map/gather | solution.py:102
  13.5 3.3 %broadcast_select_fusion = bf16[2,16,36864]{2,1,0:T(8,128)(2,1)} fusion(bf16[2,16,36864]{2,1,0:T(8,128)(2,1)} %bitcast.62, pred[2,16]{1,0:T(4,128)(4,1)S(1)} %fusion.20), kind=kLoop, calls=%fused_computation.15 | loop fusion | flops 1179648 | bytes 4718624 | tf_op jit(solution)/shard_map/jit(_where)/select_n | solution.py:102
  16.8 0.0 copy-start.7
  16.8 0.0 copy-start.8
  16.8 0.0 copy-start.5
  16.8 0.0 copy-start.4
  16.8 4.3 %all-to-all-start = ((bf16[2,16,36864]{2,1,0:T(8,128)(2,1)}), bf16[2,16,36864]{2,1,0:T(8,128)(2,1)S(1)}, u32[]{:S(2)}, u32[]{:S(2)}) async-start(bf16[2,16,36864]{2,1,0:T(8,128)(2,1)} %broadcast_select_fusion), calls=%async_computation | async-start | bytes 4718592 | tf_op jit(solution)/shard_map/all_to_all | solution.py:103
  21.2 0.0 copy-start.6
  21.2 0.0 all-reduce.2.cloned.1.call-start
  21.2 3.1 fusion.16
  24.3 0.0 all-reduce.2.cloned.1.call-update
  24.3 0.0 all-gather.2.cloned.1.call-start
  24.4 25.5 %all-to-all-done = bf16[2,16,36864]{2,1,0:T(8,128)(2,1)S(1)} async-done(((bf16[2,16,36864]{2,1,0:T(8,128)(2,1)}), bf16[2,16,36864]{2,1,0:T(8,128)(2,1)S(1)}, u32[]{:S(2)}, u32[]{:S(2)}) %all-to-all-start) | async-done | bytes 2359328 | tf_op jit(solution)/shard_map/all_to_all | solution.py:103
  49.9 0.0 copy-start.3
  49.9 1.4 copy-done.3
  51.3 0.0 all-gather.2.cloned.1.call-update
  51.3 0.0 copy-done.7
  51.3 0.6 dynamic_slice.13
  51.9 0.0 copy-done.8
  51.9 0.6 dynamic_slice.16
  52.5 0.7 add_compare_fusion
  53.1 0.1 broadcast_in_dim.116
  53.2 0.3 broadcast_in_dim.117
  53.5 1.2 copy.40
  54.7 0.7 iota_compare_fusion.1
  55.4 0.7 broadcast_compare_fusion.3
  56.1 0.7 add_convert_fusion.1
  56.8 0.0 copy-done.5
  56.8 0.7 broadcast_compare_fusion.1
  57.5 0.1 multiply_cosine_fusion
  57.6 0.2 and_and_fusion
  57.9 0.0 copy-done.4
  57.9 0.5 fusion.9
  58.4 4.4 %pad_add_fusion = pred[128,4352]{0,1:T(8,128)(4,1)S(1)} fusion(pred[128,256]{0,1:T(8,128)(4,1)S(1)} %and_and_fusion, pred[4352]{0:T(1024)(128)(4,1)S(1)} %pad.3.clone), kind=kLoop, calls=%fused_computation.16 | loop fusion | flops 557056 | bytes 594176 | tf_op jit(solution)/shard_map/concatenate | solution.py:134
  62.8 0.4 all-reduce.2.cloned.1.call-done
  63.2 1.0 multiply_reduce_fusion
  64.3 0.9 multiply_subtract_fusion
  65.2 0.0 copy-done.6
  65.2 1.1 multiply_multiply_fusion
  66.3 0.2 copy.46
  66.5 0.2 convert_element_type.67
  66.7 1.1 fusion.29
  67.8 1.5 collective-permute-start
  69.3 0.9 broadcast_select_fusion.2
  70.2 161.1 %all-gather.2.cloned.1.call-done = bf16[8,16,36864]{2,1,0:T(8,128)(2,1)} async-done(((bf16[2,16,36864]{2,1,0:T(8,128)(2,1)}), bf16[8,16,36864]{2,1,0:T(8,128)(2,1)}) %all-gather.2.cloned.1.call-update) | async-done | bytes 9437200 | tf_op jit(solution)/shard_map/all_gather | solution.py:104
  231.3 14.7 %gather_fusion.1 = bf16[64,36864]{1,0:T(8,128)(2,1)} fusion(bf16[128,36864]{1,0:T(8,128)(2,1)} %bitcast.61, s32[1024]{0:T(1024)S(1)} %pad_clamp_fusion), kind=kCustom, calls=%fused_computation.1 | custom fusion | bytes 9437440 | tf_op jit(solution)/shard_map/gather | solution.py:107
  246.0 9.9 %squeeze_reshape.3 = bf16[4096,576]{1,0:T(8,128)(2,1)} reshape(bf16[64,36864]{1,0:T(8,128)(2,1)} %gather_fusion.1) | data formatting | bytes 9437184 | tf_op jit(solution)/shard_map/squeeze;reshape | solution.py:112
  255.9 7.6 %copy.39 = bf16[4096,576]{0,1:T(8,128)(2,1)} copy(bf16[4096,576]{1,0:T(8,128)(2,1)} %squeeze_reshape.3) | data formatting | bytes 9437184 | tf_op jit(solution)/shard_map/squeeze;reshape | solution.py:112
  263.5 0.0 collective-permute-done
  263.5 5.1 %pad_maximum_fusion = bf16[4352,576]{0,1:T(8,128)(2,1)} fusion(bf16[128,576]{0,1:T(8,128)(2,1)S(1)} %get-tuple-element.2, bf16[128,576]{0,1:T(8,128)(2,1)S(1)} %bitcast.66, bf16[4096,576]{0,1:T(8,128)(2,1)} %copy.39), kind=kLoop, calls=%fused_computation.11 | loop fusion | flops 15040512 | bytes 10027008 | tf_op jit(solution)/shard_map/concatenate | solution.py:112
  268.7 0.0 copy-done.2
  268.7 11.0 %fusion.6 = f32[4352,128,8]{1,0,2:T(8,128)} fusion(bf16[128,8,32]{0,2,1:T(8,128)(2,1)S(1)} %get-tuple-element.7, bf16[128,8,32]{0,2,1:T(8,128)(2,1)S(1)} %get-tuple-element.6, bf16[128,8,512]{0,2,1:T(8,128)(2,1)S(1)} %fusion.9, bf16[128,576]{0,1:T(8,128)(2,1)S(1)} %get-tuple-element.2, bf16[128,576]{0,1:T(8,128)(2,1)S(1)} %bitcast.67, ...), kind=kOutput, calls=%fused_computation.12 | convolution fusion | flops 5152407552 | bytes 24018944 | tf_op jit(solution)/shard_map/thk,jk->htj/dot_general | solution.py:125
  279.7 22.9 %fusion.25 = (f32[8,128]{1,0:T(8,128)S(1)}, f32[8,128,4352]{1,2,0:T(8,128)}) fusion(f32[4352,128,8]{1,0,2:T(8,128)} %fusion.6, pred[128,4352]{0,1:T(8,128)(4,1)S(1)} %pad_add_fusion), kind=kOutput, calls=%fused_computation.74 | output fusion | flops 26743040 | bytes 36212736 | tf_op jit(solution)/shard_map/sub | solution.py:137
  302.6 12.8 %fusion.10 = bf16[8,128,128]{1,2,0:T(8,128)(2,1)S(1)} fusion(bf16[8,512,128]{2,1,0:T(8,128)(2,1)} %param.16, f32[8,128,4352]{1,2,0:T(8,128)} %get-tuple-element.13, f32[8,128]{1,0:T(8,128)S(1)} %get-tuple-element.12, bf16[4352,576]{0,1:T(8,128)(2,1)} %pad_maximum_fusion), kind=kOutput, calls=%fused_computation.20 | convolution fusion | flops 4707057664 | bytes 23597056 | tf_op jit(solution)/shard_map/wsd,sdp->wsp/dot_general | solution.py:142
  315.3 0.1 copy.45
  315.5 0.8 select_convert_fusion
  316.3 0.0 copy-done.1
  (16 shorter events, 0.2 us)
Async XLA Ops:
  7.2 2.8 copy-start
  16.8 34.5 %copy-start.7 = (s32[2]{0:T(128)S(1)}, s32[2]{0:T(128)}, u32[]{:S(2)}) copy-start(s32[2]{0:T(128)} %param.21) | copy-start | bytes 28
  16.8 35.1 %copy-start.8 = (s32[2]{0:T(128)S(1)}, s32[2]{0:T(128)}, u32[]{:S(2)}) copy-start(s32[2]{0:T(128)} %param.20) | copy-start | bytes 28
  16.8 39.9 %copy-start.5 = (s32[2,64,1]{1,2,0:T(1,128)S(1)}, s32[2,64,1]{1,2,0:T(1,128)}, u32[]{:S(2)}) copy-start(s32[2,64,1]{1,2,0:T(1,128)} %param.18) | copy-start | bytes 1540
  16.8 41.1 %copy-start.4 = (bf16[8,128,512]{2,1,0:T(8,128)(2,1)S(1)}, bf16[8,128,512]{2,1,0:T(8,128)(2,1)}, u32[]{:S(2)}) copy-start(bf16[8,128,512]{2,1,0:T(8,128)(2,1)} %param.15) | copy-start | bytes 3145732
  16.8 33.1 %all-to-all-start = ((bf16[2,16,36864]{2,1,0:T(8,128)(2,1)}), bf16[2,16,36864]{2,1,0:T(8,128)(2,1)S(1)}, u32[]{:S(2)}, u32[]{:S(2)}) async-start(bf16[2,16,36864]{2,1,0:T(8,128)(2,1)} %broadcast_select_fusion), calls=%async_computation | async-start | bytes 4718592 | tf_op jit(solution)/shard_map/all_to_all | solution.py:103
  21.2 44.0 %copy-start.6 = (f32[512]{0:T(512)S(1)}, f32[512]{0:T(512)}, u32[]{:S(2)}) copy-start(f32[512]{0:T(512)} %param.14) | copy-start | bytes 6148
  21.2 42.1 %all-reduce.2.cloned.1.call-start = ((), (), s32[]{:S(2)}) async-start(), calls=%async_computation.2 | async-start | bytes 589824 | tf_op jit(solution)/shard_map/psum | solution.py:83
  24.3 207.0 %all-gather.2.cloned.1.call-start = ((), (), s32[]{:S(2)}) async-start(), calls=%async_computation.1 | async-start | bytes 11796480 | tf_op jit(solution)/shard_map/all_gather | solution.py:104
  49.9 1.4 copy-start.3
  67.8 195.7 %collective-permute-start = (bf16[1,128,576]{1,2,0:T(8,128)(2,1)S(1)}, bf16[1,128,576]{1,2,0:T(8,128)(2,1)S(1)}, u32[]{:S(2)}, u32[]{:S(2)}) collective-permute-start(bf16[1,128,576]{1,2,0:T(8,128)(2,1)S(1)} %maximum_select_fusion), channel_id=1, source_target_pairs={{0,1},{2,3},{4,5},{6,7},{8,9},{10,11},{12,13},{14,15},{16,17},{18,... | collective-permute-start | bytes 442376 | tf_op jit(solution)/shard_map/ppermute | solution.py:10
  263.5 5.1 %copy-start.2 = (bf16[4096,576]{0,1:T(8,128)(2,1)S(1)}, bf16[4096,576]{0,1:T(8,128)(2,1)}, u32[]{:S(2)}) copy-start(bf16[4096,576]{0,1:T(8,128)(2,1)} %copy.39) | copy-start | bytes 14155780
  302.6 13.7 %copy-start.1 = (bf16[32,36864]{1,0:T(8,128)(2,1)S(1)}, bf16[32,36864]{1,0:T(8,128)(2,1)}, u32[]{:S(2)}) copy-start(bf16[32,36864]{1,0:T(8,128)(2,1)} %param.17) | copy-start | bytes 7077892
Sparse Core Ops, SparseCore 0:
  24.5 38.7 all-reduce.1
  64.8 166.4 all-gather.1
where the time goes:
time: 324 us; the launch traced here: 323 us
  waiting for transfers between devices  187 us (58%)
  other arithmetic  48 us (15%)
  local copies, waits for them, and re-layouts  40.5 us (12%)
  matrix products  27.4 us (8%)
  between operations  14.3 us (4%)
  starting transfers between devices  5.87 us (2%)
    all_gather x1, waiting for transfers between devices, local(): received = lax.all_gather(arrived, 'head', axis=0, tiled=True)  161 us
    all_to_all x1, waiting for transfers between devices, local(): lax.all_to_all(outgoing, 'req', split_axis=0, concat_axis=0, tiled=True)  25.5 us
    sub x1, other arithmetic, local(): exponent = jnp.exp(scores - row_max)  22.9 us
    another operation x2, local copies, waits for them, and re-layouts, local(): cached[0]  17.5 us
    gather x1, local copies, waits for them, and re-layouts, local(): received.reshape(owners * slot_cap, page_width)  14.7 us
    dot_general x1, matrix products, local(): jnp.einsum('wsd,sdp->wsp', output_latent, value_up_weight, preferred_elem...  12.8 us
    dot_general x1, matrix products, local(): jnp.einsum('thk,jk->htj', q_full, key_latent, preferred_element_type=jnp....  11 us
  transfers between devices with their start and end apart: 4, of which 3 were waited for; matrix products, arithmetic and copies ran while one was open for 16% of the time, Pallas kernels for 0%

commit v1 on v0

--- a/solution.py
+++ b/solution.py
@@ -99,12 +99,17 @@
     )
     chosen = jnp.sum(jnp.where(picked, page_slot[:, None, :], 0), axis=2)
     present = jnp.any(picked, axis=2)
-    outgoing = jnp.where(present[:, :, None], page_pool[chosen], jnp.zeros((), page_pool.dtype))
+    n_seq = lax.axis_size("seq")
+    part_width = page_width // n_seq
+    part_pool = lax.dynamic_slice_in_dim(page_pool, seq_idx * part_width, part_width, axis=1)
+    outgoing = jnp.where(present[:, :, None], part_pool[chosen], jnp.zeros((), page_pool.dtype))
     arrived = lax.all_to_all(outgoing, "req", split_axis=0, concat_axis=0, tiled=True)
-    received = lax.all_gather(arrived, "head", axis=0, tiled=True)
+    received = lax.all_gather(arrived, ("head", "seq"), axis=0, tiled=False)
+    received = received.reshape(n_head, n_seq, n_req * slot_cap, part_width)
+    received = jnp.swapaxes(received, 1, 2).reshape(owners * slot_cap, n_seq, part_width)
     own_owner = lax.dynamic_index_in_dim(owner_rows, req_idx, 0, keepdims=False)
     own_rank = lax.dynamic_index_in_dim(owner_rank, req_idx, 0, keepdims=False)
-    cached = received.reshape(owners * slot_cap, page_width)[own_owner * slot_cap + own_rank]
+    cached = received[own_owner * slot_cap + own_rank]
     prefix_width = pages_req * page_len
     cached = cached.reshape(req_dev, prefix_width, lat_width)
     key_places = jnp.arange(prefix_width, dtype=jnp.int32)

time: 324 us -> 260 us (0.80)
  waiting for transfers between devices: 187 us -> 97 us
  local copies, waits for them, and re-layouts: 40.5 us -> 66.9 us
    all_gather x1, waiting for transfers between devices: 161 us -> 0.01 us  [local(): received = lax.all_gather(arrived, ('head', 'seq'), axis=0, tiled=False)]
    psum x1, waiting for transfers between devices: 0.44 us -> 84.2 us  [local(): summed = lax.psum(partial_value, 'head')]
    reshape x0 -> x1, local copies, waits for them, and re-layouts: none -> 18.3 us  [local(): jnp.swapaxes(received, 1, 2).reshape(owners * slot_cap, n_seq, part_width)]
    all_to_all x1, waiting for transfers between devices: 25.5 us -> 12.8 us  [local(): lax.all_to_all(outgoing, 'req', split_axis=0, concat_axis=0, tiled=True)]
    transpose x0 -> x1, local copies, waits for them, and re-layouts: none -> 8.32 us  [local(): jnp.swapaxes(received, 1, 2).reshape(owners * slot_cap, n_seq, part_width)]
  transfers between devices with their start and end apart: 4 -> 4, of which waited for: 3 -> 2; matrix products, arithmetic and copies ran while one was open for 16% -> 31% of each run, Pallas kernels for 0% -> 0%
where the time goes in v1:
time: 260 us; the launch traced here: 259 us
  waiting for transfers between devices  97 us (37%)
  local copies, waits for them, and re-layouts  66.9 us (26%)
  other arithmetic  45.8 us (18%)
  matrix products  27.3 us (10%)
  between operations  15.8 us (6%)
  starting transfers between devices  6.08 us (2%)
    psum x1, waiting for transfers between devices, local(): summed = lax.psum(partial_value, 'head')  84.2 us
    sub x1, other arithmetic, local(): exponent = jnp.exp(scores - row_max)  22.8 us
    another operation x2, local copies, waits for them, and re-layouts, local(): cached[0]  19.9 us
    reshape x1, local copies, waits for them, and re-layouts, local(): jnp.swapaxes(received, 1, 2).reshape(owners * slot_cap, n_seq, part_width)  18.3 us
    gather x1, local copies, waits for them, and re-layouts, local(): cached = received[own_owner * slot_cap + own_rank]  15.5 us
    all_to_all x1, waiting for transfers between devices, local(): lax.all_to_all(outgoing, 'req', split_axis=0, concat_axis=0, tiled=True)  12.8 us
    dot_general x1, matrix products, local(): jnp.einsum('wsd,sdp->wsp', output_latent, value_up_weight, preferred_elem...  12.8 us
    dot_general x1, matrix products, local(): jnp.einsum('thk,jk->htj', q_full, key_latent, preferred_element_type=jnp....  11.1 us
  transfers between devices with their start and end apart: 4, of which 2 were waited for; matrix products, arithmetic and copies ran while one was open for 31% of the time, Pallas kernels for 0%

profile of v1, /device:TPU:0, one launch (start us, length us, event | category | flops | bytes accessed | tf_op | source)
XLA Modules:
  0.0 258.9 jit_solution(3708722827554360749)
XLA Ops:
  8.0 0.0 copy-start
  8.0 0.8 broadcast_compare_fusion.2
  8.9 0.9 convert_reduce_fusion
  9.8 0.1 fusion.20
  9.9 0.8 select_reduce_fusion
  10.7 0.1 reshape.336
  10.8 0.0 copy-done
  10.8 0.1 constant_dynamic-slice_fusion.2
  10.9 1.3 gather_fusion
  12.2 0.0 copy-start.5
  12.3 0.0 copy-start.9
  12.3 0.0 copy-start.10
  12.3 0.0 copy-start.6
  12.3 0.0 copy-start.7
  12.3 0.0 copy-start.4
  12.3 1.2 broadcast_select_fusion
  13.5 4.2 %all-to-all-start = ((bf16[2,16,18432]{2,1,0:T(8,128)(2,1)}), bf16[2,16,18432]{2,1,0:T(8,128)(2,1)S(1)}, u32[]{:S(2)}, u32[]{:S(2)}) async-start(bf16[2,16,18432]{2,1,0:T(8,128)(2,1)} %broadcast_select_fusion), calls=%async_computation | async-start | bytes 2359296 | tf_op jit(solution)/shard_map/all_to_all | solution.py:106
  17.7 0.0 all-reduce.2.cloned.1.call-start
  17.7 0.0 copy-done.5
  17.7 3.0 %fusion.16 = f32[128,576]{0,1:T(8,128)} fusion(bf16[1792,576]{0,1:T(8,128)(2,1)} %param.13, bf16[1,128,1792]{2,1,0:T(8,128)(2,1)S(1)} %copy-done.5), kind=kOutput, calls=%fused_computation.27 | convolution fusion | flops 264241152 | bytes 2818048 | tf_op jit(solution)/shard_map/dot_general | solution.py:80
  20.7 0.0 all-reduce.2.cloned.1.call-update
  20.7 0.0 all-gather.3.cloned.1.call-start
  20.8 12.8 %all-to-all-done = bf16[2,16,18432]{2,1,0:T(8,128)(2,1)S(1)} async-done(((bf16[2,16,18432]{2,1,0:T(8,128)(2,1)}), bf16[2,16,18432]{2,1,0:T(8,128)(2,1)S(1)}, u32[]{:S(2)}, u32[]{:S(2)}) %all-to-all-start) | async-done | bytes 1179680 | tf_op jit(solution)/shard_map/all_to_all | solution.py:106
  33.6 1.0 copy-done.3
  34.6 0.0 all-gather.3.cloned.1.call-update
  34.6 0.0 copy-done.9
  34.6 0.6 dynamic_slice.16
  35.2 0.6 dynamic_slice.20
  35.8 0.7 add_compare_fusion
  36.5 0.1 broadcast_in_dim.116
  36.5 0.3 broadcast_in_dim.117
  36.8 0.2 copy.57
  37.1 0.7 iota_compare_fusion.1
  37.7 0.7 broadcast_compare_fusion.3
  38.4 0.7 add_convert_fusion.1
  39.1 0.0 copy-done.7
  39.1 0.7 broadcast_compare_fusion.1
  39.8 0.1 multiply_cosine_fusion
  39.9 0.2 and_and_fusion
  40.2 0.0 copy-done.4
  40.2 0.5 fusion.9
  40.7 4.4 %pad_add_fusion = pred[128,4352]{0,1:T(8,128)(4,1)S(1)} fusion(pred[128,256]{0,1:T(8,128)(4,1)S(1)} %and_and_fusion, pred[4352]{0:T(1024)(128)(4,1)S(1)} %pad.3.clone), kind=kLoop, calls=%fused_computation.15 | loop fusion | flops 557056 | bytes 594176 | tf_op jit(solution)/shard_map/concatenate | solution.py:139
  45.1 84.2 %all-reduce.2.cloned.1.call-done = f32[128,576]{0,1:T(8,128)} async-done(((f32[128,576]{0,1:T(8,128)}), f32[128,576]{0,1:T(8,128)}) %all-reduce.2.cloned.1.call-update) | async-done | bytes 294928 | tf_op jit(solution)/shard_map/psum | solution.py:83
  129.3 1.0 multiply_reduce_fusion
  130.3 0.9 multiply_subtract_fusion
  131.2 0.0 copy-done.8
  131.2 1.1 multiply_multiply_fusion
  132.4 0.2 copy.63
  132.5 0.2 convert_element_type.67
  132.7 1.1 fusion.33
  133.9 1.8 collective-permute-start
  135.7 0.9 broadcast_select_fusion.2
  136.6 8.3 %copy.54 = bf16[4,32,2,18432]{3,1,0,2:T(8,128)(2,1)} copy(bf16[4,32,2,18432]{3,1,2,0:T(8,128)(2,1)} %bitcast.71) | data formatting | bytes 18874368 | tf_op jit(solution)/shard_map/transpose | solution.py:109
  144.9 18.3 %copy.55 = bf16[128,2,18432]{2,1,0:T(2,128)(2,1)} copy(bf16[128,2,18432]{2,0,1:T(8,128)(2,1)} %bitcast.70) | data formatting | bytes 18874368 | tf_op jit(solution)/shard_map/reshape | solution.py:109
  163.2 15.5 %gather_fusion.1 = bf16[64,2,18432]{2,1,0:T(2,128)(2,1)} fusion(bf16[128,2,18432]{2,1,0:T(2,128)(2,1)} %copy.55, s32[1024]{0:T(1024)S(1)} %pad_clamp_fusion), kind=kCustom, calls=%fused_computation.1 | custom fusion | bytes 9437440 | tf_op jit(solution)/shard_map/gather | solution.py:112
  178.8 12.3 %squeeze_reshape.3 = bf16[4096,576]{1,0:T(8,128)(2,1)} reshape(bf16[64,2,18432]{2,1,0:T(2,128)(2,1)} %gather_fusion.1) | data formatting | bytes 9437184 | tf_op jit(solution)/shard_map/squeeze;reshape | solution.py:117
  191.1 7.6 %copy.56 = bf16[4096,576]{0,1:T(8,128)(2,1)} copy(bf16[4096,576]{1,0:T(8,128)(2,1)} %squeeze_reshape.3) | data formatting | bytes 9437184 | tf_op jit(solution)/shard_map/squeeze;reshape | solution.py:117
  198.7 0.0 collective-permute-done
  198.7 5.1 %pad_maximum_fusion = bf16[4352,576]{0,1:T(8,128)(2,1)} fusion(bf16[128,576]{0,1:T(8,128)(2,1)S(1)} %get-tuple-element.2, bf16[128,576]{0,1:T(8,128)(2,1)S(1)} %bitcast.76, bf16[4096,576]{0,1:T(8,128)(2,1)} %copy.56), kind=kLoop, calls=%fused_computation.11 | loop fusion | flops 15040512 | bytes 10027008 | tf_op jit(solution)/shard_map/concatenate | solution.py:117
  203.8 11.1 %fusion.6 = f32[4352,128,8]{1,0,2:T(8,128)} fusion(bf16[128,8,32]{0,2,1:T(8,128)(2,1)S(1)} %get-tuple-element.7, bf16[128,8,32]{0,2,1:T(8,128)(2,1)S(1)} %get-tuple-element.6, bf16[128,8,512]{0,2,1:T(8,128)(2,1)S(1)} %fusion.9, bf16[128,576]{0,1:T(8,128)(2,1)S(1)} %get-tuple-element.2, bf16[128,576]{0,1:T(8,128)(2,1)S(1)} %bitcast.77, ...), kind=kOutput, calls=%fused_computation.12 | convolution fusion | flops 5152407552 | bytes 24018944 | tf_op jit(solution)/shard_map/thk,jk->htj/dot_general | solution.py:130
  214.9 22.8 %fusion.29 = (f32[8,128]{1,0:T(8,128)S(1)}, f32[8,128,4352]{1,2,0:T(8,128)}) fusion(f32[4352,128,8]{1,0,2:T(8,128)} %fusion.6, pred[128,4352]{0,1:T(8,128)(4,1)S(1)} %pad_add_fusion), kind=kOutput, calls=%fused_computation.80 | output fusion | flops 26743040 | bytes 36212736 | tf_op jit(solution)/shard_map/sub | solution.py:142
  237.7 12.8 %fusion.10 = bf16[8,128,128]{1,2,0:T(8,128)(2,1)S(1)} fusion(bf16[8,512,128]{2,1,0:T(8,128)(2,1)} %param.16, f32[8,128,4352]{1,2,0:T(8,128)} %get-tuple-element.13, f32[8,128]{1,0:T(8,128)S(1)} %get-tuple-element.12, bf16[4352,576]{0,1:T(8,128)(2,1)} %pad_maximum_fusion), kind=kOutput, calls=%fused_computation.19 | convolution fusion | flops 4707057664 | bytes 23597056 | tf_op jit(solution)/shard_map/wsd,sdp->wsp/dot_general | solution.py:147
  250.5 0.1 copy.62
  250.6 0.8 select_convert_fusion
  (23 shorter events, 0.2 us)
Async XLA Ops:
  8.0 2.8 %copy-start = (bf16[32,36864]{1,0:T(8,128)(2,1)S(1)}, bf16[32,36864]{1,0:T(8,128)(2,1)}, u32[]{:S(2)}) copy-start(bf16[32,36864]{1,0:T(8,128)(2,1)} %param.17) | copy-start | bytes 7077892
  12.2 5.5 %copy-start.5 = (bf16[1,128,1792]{2,1,0:T(8,128)(2,1)S(1)}, bf16[1,128,1792]{2,1,0:T(8,128)(2,1)}, u32[]{:S(2)}) copy-start(bf16[1,128,1792]{2,1,0:T(8,128)(2,1)} %param.12) | copy-start | bytes 1376260
  12.3 22.4 %copy-start.9 = (s32[2]{0:T(128)S(1)}, s32[2]{0:T(128)}, u32[]{:S(2)}) copy-start(s32[2]{0:T(128)} %param.21) | copy-start | bytes 28
  12.3 22.9 %copy-start.10 = (s32[2]{0:T(128)S(1)}, s32[2]{0:T(128)}, u32[]{:S(2)}) copy-start(s32[2]{0:T(128)} %param.20) | copy-start | bytes 28
  12.3 24.6 %copy-start.6 = (bf16[1,128,1536]{2,1,0:T(8,128)(2,1)S(1)}, bf16[1,128,1536]{2,1,0:T(8,128)(2,1)}, u32[]{:S(2)}) copy-start(bf16[1,128,1536]{2,1,0:T(8,128)(2,1)} %param.11) | copy-start | bytes 1179652
  12.3 26.8 %copy-start.7 = (s32[2,64,1]{1,2,0:T(1,128)S(1)}, s32[2,64,1]{1,2,0:T(1,128)}, u32[]{:S(2)}) copy-start(s32[2,64,1]{1,2,0:T(1,128)} %param.18) | copy-start | bytes 1540
  12.3 27.9 %copy-start.4 = (bf16[8,128,512]{2,1,0:T(8,128)(2,1)S(1)}, bf16[8,128,512]{2,1,0:T(8,128)(2,1)}, u32[]{:S(2)}) copy-start(bf16[8,128,512]{2,1,0:T(8,128)(2,1)} %param.15) | copy-start | bytes 3145732
  13.5 20.1 %all-to-all-start = ((bf16[2,16,18432]{2,1,0:T(8,128)(2,1)}), bf16[2,16,18432]{2,1,0:T(8,128)(2,1)S(1)}, u32[]{:S(2)}, u32[]{:S(2)}) async-start(bf16[2,16,18432]{2,1,0:T(8,128)(2,1)} %broadcast_select_fusion), calls=%async_computation | async-start | bytes 2359296 | tf_op jit(solution)/shard_map/all_to_all | solution.py:106
  17.7 113.5 %copy-start.8 = (f32[512]{0:T(512)S(1)}, f32[512]{0:T(512)}, u32[]{:S(2)}) copy-start(f32[512]{0:T(512)} %param.14) | copy-start | bytes 6148
  17.7 111.6 %all-reduce.2.cloned.1.call-start = ((), (), s32[]{:S(2)}) async-start(), calls=%async_computation.1 | async-start | bytes 589824 | tf_op jit(solution)/shard_map/psum | solution.py:83
  20.7 115.9 %all-gather.3.cloned.1.call-start = ((), (), s32[]{:S(2)}) async-start(), calls=%async_computation.2 | async-start | bytes 10616832 | tf_op jit(solution)/shard_map/all_gather | solution.py:107
  33.6 1.0 copy-start.3
  133.9 64.8 %collective-permute-start = (bf16[1,128,576]{1,2,0:T(8,128)(2,1)S(1)}, bf16[1,128,576]{1,2,0:T(8,128)(2,1)S(1)}, u32[]{:S(2)}, u32[]{:S(2)}) collective-permute-start(bf16[1,128,576]{1,2,0:T(8,128)(2,1)S(1)} %maximum_select_fusion), channel_id=1, source_target_pairs={{0,1},{2,3},{4,5},{6,7},{8,9},{10,11},{12,13},{14,15},{16,17},{18,... | collective-permute-start | bytes 442376 | tf_op jit(solution)/shard_map/ppermute | solution.py:10
  198.7 5.1 %copy-start.2 = (bf16[4096,576]{0,1:T(8,128)(2,1)S(1)}, bf16[4096,576]{0,1:T(8,128)(2,1)}, u32[]{:S(2)}) copy-start(bf16[4096,576]{0,1:T(8,128)(2,1)} %copy.56) | copy-start | bytes 14155780
  237.7 13.7 %copy-start.1 = (bf16[32,36864]{1,0:T(8,128)(2,1)S(1)}, bf16[32,36864]{1,0:T(8,128)(2,1)}, u32[]{:S(2)}) copy-start(bf16[32,36864]{1,0:T(8,128)(2,1)} %param.17) | copy-start | bytes 7077892
Sparse Core Ops, SparseCore 0:
  20.9 108.3 all-reduce.1
Sparse Core Ops, SparseCore 1:
  34.7 94.5 all-gather.2

commit v2 on v0

v2 whole, which is shorter than its diff:
```python
import functools
import math

import jax
import jax.numpy as jnp
from jax import lax
from jax.experimental import pallas as pl
from jax.experimental.pallas import tpu as pltpu
from jax.sharding import PartitionSpec as P

LOWEST = -1e30
VMEM_LIMIT = 48 * 1024 * 1024


def from_behind(block, axis, distance):
    devices = range(lax.axis_size(axis))
    route = [(i - distance, i) for i in devices if i - distance in devices]
    return lax.ppermute(block, axis, route)


def rotate(vector, cosine_table, sine_table):
    half_width = vector.shape[-1] // 2
    first_half = vector[..., :half_width]
    second_half = vector[..., half_width:]
    return jnp.concatenate(
        [
            first_half * cosine_table - second_half * sine_table,
            first_half * sine_table + second_half * cosine_table,
        ],
        axis=-1,
    )


def angles(positions, rope_width):
    half_width = rope_width // 2
    frequency = 10000.0 ** (-2.0 * jnp.arange(half_width, dtype=jnp.float32) / rope_width)
    phases = positions.astype(jnp.float32)[:, None] * frequency[None, :]
    return (jnp.cos(phases), jnp.sin(phases))


def finish_latent(summed, positions, live_rows, kv_gain, latent_width):
    latent_part = summed[:, :latent_width]
    mean_square = jnp.mean(latent_part * latent_part, axis=-1, keepdims=True)
    normed = latent_part * lax.rsqrt(mean_square + 1e-06) * kv_gain
    cosine_table, sine_table = angles(positions, summed.shape[1] - latent_width)
    rotated = rotate(summed[:, latent_width:], cosine_table, sine_table)
    joined = jnp.concatenate([normed, rotated], axis=-1).astype(jnp.bfloat16)
    return jnp.where(live_rows[:, None], joined, jnp.zeros_like(joined))


def any_spec():
    return pl.BlockSpec(memory_space=pl.ANY)


def smem_spec():
    return pl.BlockSpec(memory_space=pltpu.SMEM)


def vmem_spec():
    return pl.BlockSpec(memory_space=pltpu.VMEM)


def pick_kernel(cap, owner_ref, slot_ref, pool_ref, count_ref, own_ref, foreign_ref, pages, lists, sems):
    n_req = lax.axis_size("req")
    head_idx = lax.axis_index("head")
    req_idx = lax.axis_index("req")
    seq_idx = lax.axis_index("seq")
    n_pages = owner_ref.shape[1]
    pool_pages, pairs, pair_width = pages.shape
    step = 16
    row = lax.broadcasted_iota(jnp.int32, (step * step, step * step), 0)
    column = lax.broadcasted_iota(jnp.int32, (step * step, step * step), 1)
    swap = ((row // step == column % step) & (row % step == column // step)).astype(jnp.bfloat16)
    for page in range(0, pool_pages, step):
        for pair in range(0, pairs, step):
            rows = jnp.concatenate(
                [
                    pool_ref[page : page + step, (pair + i) * pair_width : (pair + i + 1) * pair_width]
                    for i in range(step)
                ],
                axis=0,
            )
            turned = jnp.dot(swap, rows, preferred_element_type=jnp.float32).astype(jnp.bfloat16)
            pages[page : page + step, pair : pair + step, :] = turned.reshape(step, step, pair_width)
    self_owner = head_idx * n_req + req_idx
    for shift in range(n_req):
        request = lax.rem(req_idx + shift, n_req)

        def note(page, found, shift=shift, request=request):
            lists[shift, found] = slot_ref[request, page]
            return found + (owner_ref[request, page] == self_owner).astype(jnp.int32)

        found = lax.fori_loop(0, n_pages, note, jnp.int32(0), unroll=8)
        ranks = cap if shift == 0 else foreign_ref.shape[1]
        first = 0 if shift == 0 else seq_idx * ranks
        for j in range(ranks):
            rank = first + j
            slot = jnp.where(rank < found, lists[shift, rank], 0)
            target = own_ref.at[j] if shift == 0 else foreign_ref.at[shift - 1, j]
            pltpu.make_async_copy(pages.at[slot], target, sems.at[min(shift, 1)]).start()

    def tally(page, counts):
        owner = owner_ref[req_idx, page]
        return tuple(
            counts[shift]
            + (owner == head_idx * n_req + lax.rem(req_idx + n_req - shift, n_req)).astype(jnp.int32)
            for shift in range(n_req)
        )

    counts = lax.fori_loop(0, n_pages, tally, (jnp.int32(0),) * n_req, unroll=8)
    for shift in range(n_req):
        count_ref[shift] = counts[shift]
    pltpu.make_async_copy(own_ref, own_ref, sems.at[0]).wait()
    pltpu.make_async_copy(foreign_ref, foreign_ref, sems.at[1]).wait()


def pick_pages(page_owner, page_slot, page_pool, cap, n_req, n_seq, pairs):
    pool_pages, page_width = page_pool.shape
    pair_width = page_width // pairs
    page = (pairs, pair_width)
    return pl.pallas_call(
        functools.partial(pick_kernel, cap),
        out_shape=(
            jax.ShapeDtypeStruct((n_req,), jnp.int32),
            jax.ShapeDtypeStruct((cap, *page), jnp.bfloat16),
            jax.ShapeDtypeStruct((n_req - 1, cap // n_seq, *page), jnp.bfloat16),
        ),
        in_specs=[smem_spec(), smem_spec(), vmem_spec()],
        out_specs=(smem_spec(), any_spec(), any_spec()),
        scratch_shapes=[
            pltpu.VMEM((pool_pages, *page), jnp.bfloat16),
            pltpu.SMEM((n_req, cap + 1), jnp.int32),
            pltpu.SemaphoreType.DMA((2,)),
        ],
        compiler_params=pltpu.CompilerParams(vmem_limit_bytes=VMEM_LIMIT),
        cost_estimate=pl.CostEstimate(flops=10**9, bytes_accessed=6 * 10**6, transcendentals=0),
        name="pick_pages",
    )(page_owner, page_slot, page_pool)


def join_kernel(chunk, count_ref, own_ref, mine_ref, other_ref, joined_ref, first_ref, second_ref, sems):
    seq_idx = lax.axis_index("seq")
    n_req = count_ref.shape[0]
    half_cap = mine_ref.shape[1]
    for j in range(joined_ref.shape[0]):
        targets = [(joined_ref.at[j], sems.at[0])]
        if j < chunk:
            targets.append((first_ref.at[j], sems.at[1]))
        elif j < 2 * chunk:
            targets.append((second_ref.at[j - chunk], sems.at[2]))

        def fetch(condition, source):
            @pl.when(condition)
            def _():
                for target, sem in targets:
                    pltpu.make_async_copy(source, target, sem).start()

        rank = jnp.int32(j)
        taken = rank < count_ref[0]
        fetch(taken, own_ref.at[jnp.minimum(rank, own_ref.shape[0] - 1)])
        rank = rank - count_ref[0]
        for shift in range(1, n_req):
            here = jnp.logical_not(taken) & (rank < count_ref[shift])
            place = jnp.clip(lax.rem(rank, half_cap), 0, half_cap - 1)
            local = rank // half_cap == seq_idx
            fetch(here & local, mine_ref.at[shift - 1, place])
            fetch(here & jnp.logical_not(local), other_ref.at[shift - 1, place])
            taken = taken | here
            rank = rank - count_ref[shift]
        fetch(jnp.logical_not(taken), own_ref.at[0])
    for i, ref in enumerate((joined_ref, first_ref, second_ref)):
        pltpu.make_async_copy(ref, ref, sems.at[i]).wait()


def join_pages(counts, own, mine, other, chunk):
    page = own.shape[1:]
    return pl.pallas_call(
        functools.partial(join_kernel, chunk),
        out_shape=(
            jax.ShapeDtypeStruct((4 * chunk, *page), jnp.bfloat16),
            jax.ShapeDtypeStruct((chunk, *page), jnp.bfloat16),
            jax.ShapeDtypeStruct((chunk, *page), jnp.bfloat16),
        ),
        in_specs=[smem_spec(), any_spec(), any_spec(), any_spec()],
        out_specs=(any_spec(), any_spec(), any_spec()),
        scratch_shapes=[pltpu.SemaphoreType.DMA((3,))],
        cost_estimate=pl.CostEstimate(flops=0, bytes_accessed=6 * 10**6, transcendentals=0),
        name="join_pages",
    )(counts, own, mine, other)


def queue_kernel(step, chunk, earliest, held_ref, joined_ref, *refs):
    arrived, target_ref, sem = refs[:-2], refs[-2], refs[-1]
    held = held_ref[0]
    offset = jnp.maximum(held, 2 * chunk)
    for j in range(chunk):
        entry = step * chunk + j

        def fetch(condition, source, j=j):
            @pl.when(condition)
            def _():
                pltpu.make_async_copy(source, target_ref.at[j], sem).start()

        taken = entry < held
        if entry < joined_ref.shape[0]:
            fetch(taken, joined_ref.at[entry])
        place = entry - offset - earliest * chunk
        for i, source in enumerate(arrived):
            here = (place >= i * chunk) & (place < (i + 1) * chunk)
            fetch(here, source.at[jnp.clip(place - i * chunk, 0, chunk - 1)])
            taken = taken | here
        fetch(jnp.logical_not(taken), joined_ref.at[0])
    pltpu.make_async_copy(target_ref, target_ref, sem).wait()


def queue_chunk(step, held, joined, arrived):
    chunk = joined.shape[0] // 4
    earliest = max(0, step - 4)
    sources = arrived[earliest : step - 1]
    return pl.pallas_call(
        functools.partial(queue_kernel, step, chunk, earliest),
        out_shape=jax.ShapeDtypeStruct((chunk, *joined.shape[1:]), jnp.bfloat16),
        in_specs=[smem_spec()] + [any_spec()] * (1 + len(sources)),
        out_specs=any_spec(),
        scratch_shapes=[pltpu.SemaphoreType.DMA],
        cost_estimate=pl.CostEstimate(flops=0, bytes_accessed=10**6, transcendentals=0),
        name="queue_chunk",
    )(held, joined, *sources)


def token_limits(owners, prefix, head_idx, req_idx, seq_idx, n_head, n_req, chunk, steps, page_len):
    pages = owners.shape[0]
    order = jnp.arange(pages, dtype=jnp.int32)
    place = owners // n_req
    key = lax.rem(req_idx + n_req - lax.rem(owners, n_req), n_req) * pages + order
    ahead = (place[None, :] == place[:, None]) & (key[None, :] < key[:, None])
    rank = jnp.sum(ahead.astype(jnp.int32), axis=1)
    heads = jnp.arange(n_head, dtype=jnp.int32)
    held = jnp.sum((place[None, :] == heads[:, None]).astype(jnp.int32), axis=1)
    widths = jnp.maximum(held, 2 * chunk)

    def before(position):
        return jnp.sum(jnp.where(heads[None, :] < position[:, None], widths[None, :], 0), axis=1)

    here = jnp.full((pages,), head_idx, jnp.int32)
    upward = rank + before(here) - before(place + 1)
    downward = rank + before(place) - before(here + 1)
    up_base = 4 * chunk + seq_idx * steps * chunk
    down_base = 4 * chunk + (1 - seq_idx) * steps * chunk
    slot = jnp.where(
        place == here, rank, jnp.where(place < here, up_base + upward, down_base + downward)
    )
    tokens = jnp.clip(prefix - order * page_len, 0, page_len)
    slots = jnp.arange(4 * chunk + 2 * steps * chunk, dtype=jnp.int32)
    limits = jnp.sum(jnp.where(slot[None, :] == slots[:, None], tokens[None, :], 0), axis=1)
    held_here = jnp.sum((place == here).astype(jnp.int32))
    return limits, held_here.reshape(1)


def attend_kernel(shape, first, last, *refs):
    rows, tile, scale, n_blocks, chunk, half_len = shape
    refs = list(refs)
    limit_ref, q_ref = refs.pop(0), refs.pop(0)
    state = [] if first else [refs.pop(0) for _ in range(3)]
    if last:
        suffix_ref, earlier_ref, fresh_ref, up_ref = [refs.pop(0) for _ in range(4)]
    sources = []
    total = 0
    while total < n_blocks:
        source = refs.pop(0)
        sources.append((source, source.shape[0] // chunk))
        total += sources[-1][1]
    if last:
        out_ref = refs.pop(0)
    values, highest, weight_sum, blocks, keys, sems = refs
    latent_width = values.shape[1]
    key_width = keys.shape[1]
    index = 0
    for source, count in sources:
        for i in range(count):
            pltpu.make_async_copy(
                source.at[i * chunk : (i + 1) * chunk], blocks.at[index], sems.at[index]
            ).start()
            index += 1
    if first:
        values[...] = jnp.zeros_like(values)
        highest[...] = jnp.full_like(highest, LOWEST)
        weight_sum[...] = jnp.zeros_like(weight_sum)
    else:
        values[...] = state[0][...]
        highest[...] = state[1][...]
        weight_sum[...] = state[2][...]

    def visit(key_block, mask_of):
        for start in range(0, rows, tile):
            part = slice(start, start + tile)
            scores = lax.dot_general(
                q_ref[part, :], key_block[...], (((1,), (1,)), ((), ())), preferred_element_type=jnp.float32
            )
            scores = mask_of(scores * scale, start)
            old = highest[part, :]
            new = jnp.maximum(old, jnp.max(scores, axis=1, keepdims=True))
            weights = jnp.exp2(scores - new)
            shrink = jnp.exp2(old - new)
            highest[part, :] = new
            weight_sum[part, :] = weight_sum[part, :] * shrink + jnp.sum(weights, axis=1, keepdims=True)
            values[part, :] = values[part, :] * shrink + jnp.dot(
                weights.astype(jnp.bfloat16),
                key_block[:, :latent_width],
                preferred_element_type=jnp.float32,
            )

    pairs = blocks.shape[2]
    pair_rows = chunk * pairs

    def one_block(block, carry):
        pltpu.make_async_copy(blocks.at[block], blocks.at[block], sems.at[block]).wait()
        limits = [limit_ref[block * chunk + j] for j in range(chunk)]
        some = functools.reduce(jnp.maximum, limits)

        @pl.when(some > 0)
        def _():
            page_rows = blocks[block].reshape(pair_rows, blocks.shape[3])
            keys[:pair_rows, :] = page_rows[:, :key_width]
            keys[pair_rows : 2 * pair_rows, :] = page_rows[:, key_width:]
            lane = lax.broadcasted_iota(jnp.int32, (1, 2 * pair_rows), 1)
            within = lax.rem(lane, pair_rows)
            token = 2 * lax.rem(within, pairs) + lane // pair_rows
            limit = jnp.zeros_like(lane)
            for j in range(chunk):
                limit = jnp.where(within // pairs == j, limits[j], limit)
            bias = jnp.where(token < limit, 0.0, -jnp.inf)
            visit(keys.at[: 2 * pair_rows], lambda scores, start: scores + bias)

        return carry

    lax.fori_loop(0, n_blocks, one_block, 0)
    if not last:
        return
    live = suffix_ref[0]
    seq_idx = lax.axis_index("seq")
    keys[:half_len, :] = earlier_ref[...]
    keys[half_len : 2 * half_len, :] = fresh_ref[...]

    def near(scores, start):
        row = lax.broadcasted_iota(jnp.int32, scores.shape, 0) + start
        place = lax.broadcasted_iota(jnp.int32, scores.shape, 1) + (seq_idx - 1) * half_len
        query = lax.rem(row, half_len) + seq_idx * half_len
        allowed = (place >= 0) & (place <= query) & (place < live)
        return jnp.where(allowed, scores, -jnp.inf)

    visit(keys.at[: 2 * half_len], near)
    heads, _, value_width = up_ref.shape
    steps = lax.broadcasted_iota(jnp.int32, (half_len, value_width), 0) + seq_idx * half_len
    for head in range(heads):
        part = slice(head * half_len, (head + 1) * half_len)
        latent = (values[part, :] / weight_sum[part, :]).astype(jnp.bfloat16)
        raised = jnp.dot(latent, up_ref[head], preferred_element_type=jnp.float32)
        out_ref[:, head * value_width : (head + 1) * value_width] = jnp.where(
            steps < live, raised, 0.0
        ).astype(jnp.bfloat16)


def attend(limits, q_rows, blocks, chunk, latent_width, half_len, scale, state=None, tail=None):
    rows, key_width = q_rows.shape
    pairs, pair_width = blocks[0].shape[1:]
    n_blocks = sum(b.shape[0] for b in blocks) // chunk
    block_keys = max(2 * pairs * chunk, 2 * half_len)
    state_shapes = [
        jax.ShapeDtypeStruct((rows, latent_width), jnp.float32),
        jax.ShapeDtypeStruct((rows, 1), jnp.float32),
        jax.ShapeDtypeStruct((rows, 1), jnp.float32),
    ]
    state_scratch = [pltpu.VMEM(s.shape, s.dtype) for s in state_shapes]
    scratch = [
        pltpu.VMEM((n_blocks, chunk, pairs, pair_width), jnp.bfloat16),
        pltpu.VMEM((block_keys, key_width), jnp.bfloat16),
        pltpu.SemaphoreType.DMA((n_blocks,)),
    ]
    operands = [limits, q_rows]
    specs = [smem_spec(), vmem_spec()]
    if state is not None:
        operands += list(state)
        specs += [vmem_spec()] * 3
    if tail is not None:
        operands += list(tail)
        specs += [smem_spec()] + [vmem_spec()] * 3
        heads, _, value_width = tail[-1].shape
        out_shape = jax.ShapeDtypeStruct((half_len, heads * value_width), jnp.bfloat16)
        out_specs = vmem_spec()
        scratch = state_scratch + scratch
    else:
        out_shape = tuple(state_shapes)
        out_specs = (vmem_spec(),) * 3
    operands += list(blocks)
    specs += [any_spec()] * len(blocks)
    shape = (rows, 256 if rows % 256 == 0 else rows, scale * math.log2(math.e), n_blocks, chunk, half_len)
    work = n_blocks * 2 * pairs * chunk * rows
    return pl.pallas_call(
        functools.partial(attend_kernel, shape, state is None, tail is not None),
        out_shape=out_shape,
        in_specs=specs,
        out_specs=out_specs,
        scratch_shapes=scratch,
        compiler_params=pltpu.CompilerParams(vmem_limit_bytes=VMEM_LIMIT),
        cost_estimate=pl.CostEstimate(
            flops=2 * work * (key_width + latent_width) // 2, bytes_accessed=10**7, transcendentals=work // 2
        ),
        name="attend",
    )(*operands)


def local(
    queries,
    hidden,
    w_dkv,
    kv_gain,
    w_uk,
    value_up_weight,
    page_pool,
    page_owner,
    page_slot,
    prefix_len,
    suffix_len,
):
    n_head = lax.axis_size("head")
    n_req = lax.axis_size("req")
    n_seq = lax.axis_size("seq")
    head_idx = lax.axis_index("head")
    req_idx = lax.axis_index("req")
    seq_idx = lax.axis_index("seq")
    _, half_len, d_local = hidden.shape
    heads_dev, nope_width, latent_width = w_uk.shape
    lat_width = w_dkv.shape[1]
    rope_width = lat_width - latent_width
    query_width = queries.shape[2] // heads_dev
    page_width = page_pool.shape[1]
    page_len = page_width // lat_width
    pairs = page_len // 2
    pages_req = page_slot.shape[1]
    cap = max(2, 2 * pages_req // (n_head * n_req))
    chunk = n_req * cap // 4
    steps = 3 * n_head - 2
    score_scale = float(query_width) ** (-0.5)

    owner_rows = page_owner[:, :, 0]
    counts, own, foreign = pick_pages(owner_rows, page_slot, page_pool, cap, n_req, n_seq, pairs)
    swap_route = [(i, n_seq - 1 - i) for i in range(n_seq)]
    mine = jnp.stack(
        [
            lax.ppermute(foreign[s - 1], "req", [(i, (i + s) % n_req) for i in range(n_req)])
            for s in range(1, n_req)
        ]
    )
    other = lax.ppermute(mine, "seq", swap_route)
    joined, first_chunk, second_chunk = join_pages(counts, own, mine, other, chunk)

    my_prefix = lax.dynamic_index_in_dim(prefix_len, req_idx, 0, keepdims=False)
    my_suffix = lax.dynamic_index_in_dim(suffix_len, req_idx, 0, keepdims=False)
    own_owners = lax.dynamic_index_in_dim(owner_rows, req_idx, 0, keepdims=False)
    limits, held = token_limits(
        own_owners, my_prefix, head_idx, req_idx, seq_idx, n_head, n_req, chunk, steps, page_len
    )
    local_t = jnp.arange(half_len, dtype=jnp.int32)
    glob_t = seq_idx * half_len + local_t
    positions = my_prefix + glob_t
    live_rows = glob_t < my_suffix

    partial_value = jnp.dot(hidden[0], w_dkv, preferred_element_type=jnp.float32)
    summed = lax.psum(partial_value, "head")
    fresh = finish_latent(summed, positions, live_rows, kv_gain, latent_width)
    new_pages = fresh.reshape(1, half_len // page_len, page_len * lat_width)
    earlier = from_behind(fresh, "seq", 1)

    query_rows = queries[0].reshape(half_len, heads_dev, query_width)
    q_latent = jnp.einsum(
        "thn,hnk->htk", query_rows[..., :nope_width], w_uk, preferred_element_type=jnp.float32
    ).astype(jnp.bfloat16)
    cosine_table, sine_table = angles(positions, rope_width)
    q_rotated = rotate(
        jnp.swapaxes(query_rows[..., nope_width:], 0, 1).astype(jnp.float32), cosine_table, sine_table
    ).astype(jnp.bfloat16)
    q_rows = jnp.concatenate([q_latent, q_rotated], axis=-1).reshape(heads_dev * half_len, lat_width)

    stream_route = []
    for i in range(n_head - 1):
        stream_route.append((i * n_seq, (i + 1) * n_seq))
        stream_route.append(((i + 1) * n_seq + 1, i * n_seq + 1))
    arrived, swapped = [], []
    for step in range(steps):
        if step == 0:
            outgoing = first_chunk
        elif step == 1:
            outgoing = second_chunk
        else:
            outgoing = queue_chunk(step, held, joined, arrived)
        arrived.append(lax.ppermute(outgoing, ("head", "seq"), stream_route))
        swapped.append(lax.ppermute(arrived[-1], "seq", swap_route))

    def limit_part(first, last):
        mine_base = 4 * chunk
        other_base = mine_base + steps * chunk
        return [
            limits[mine_base + first * chunk : mine_base + last * chunk],
            limits[other_base + first * chunk : other_base + last * chunk],
        ]

    run = functools.partial(
        attend, chunk=chunk, latent_width=latent_width, half_len=half_len, scale=score_scale
    )
    cuts = [0, 3 * steps // 10, 7 * steps // 10, steps]
    state = None
    for i in range(3):
        low, high = cuts[i], cuts[i + 1]
        blocks = ([joined] if i == 0 else []) + arrived[low:high] + swapped[low:high]
        part = jnp.concatenate(([limits[: 4 * chunk]] if i == 0 else []) + limit_part(low, high))
        tail = None
        if i == 2:
            tail = (my_suffix.reshape(1), earlier, fresh, value_up_weight)
        state = run(part, q_rows, blocks, state=state, tail=tail)
    return (state[None], new_pages)


def solution(mesh):
    placed = (
        P(("groups", "req"), "seq", "head"),
        P(("groups", "req"), "seq", "head"),
        P("head", None),
        P(),
        P("head", None, None),
        P("head", None, None),
        P(("groups", "head", "req"), None),
        P("groups", None, None),
        P("groups", None),
        P("groups"),
        P("groups"),
    )
    return jax.shard_map(
        local,
        mesh=mesh,
        in_specs=placed,
        out_specs=(P(("groups", "req"), "seq", "head"), P(("groups", "req"), "seq", None)),
        check_vma=False,
    )
```

time: 324 us -> 431 us (1.33)
  Pallas kernels: 0 us -> 316 us
  waiting for transfers between devices: 187 us -> 19.8 us
  starting transfers between devices: 5.87 us -> 38.6 us
  other arithmetic: 48 us -> 15.4 us
  matrix products: 27.4 us -> 4.35 us
  local copies, waits for them, and re-layouts: 40.5 us -> 20 us
    pallas_call x0 -> x13, Pallas kernels: none -> 316 us  [the longest x8 157 us: queue_chunk(): pl.pallas_call(functools.partial(queue_kernel, step, chunk, earliest), ou...]
    all_gather x1 -> x0, waiting for transfers between devices: 161 us -> none  [local(): received = lax.all_gather(arrived, 'head', axis=0, tiled=True)]
    ppermute x0 -> x22, starting transfers between devices: none -> 36.2 us  [the longest x10 30.7 us: local(): arrived.append(lax.ppermute(outgoing, ('head', 'seq'), stream_route))]
    all_to_all x1 -> x0, waiting for transfers between devices: 25.5 us -> none  [local(): lax.all_to_all(outgoing, 'req', split_axis=0, concat_axis=0, tiled=True)]
    dot_general x4 -> x2, matrix products: 27.4 us -> 4.35 us  [the longest x1 2.79 us: local(): jnp.einsum('thn,hnk->htk', query_rows[..., :nope_width], w_uk, preferred_...]
    sub x1 -> x0, other arithmetic: 22.9 us -> none  [local(): exponent = jnp.exp(scores - row_max)]
    ppermute x0 -> x22, waiting for transfers between devices: none -> 19.8 us  [the longest x10 10.4 us: local(): arrived.append(lax.ppermute(outgoing, ('head', 'seq'), stream_route))]
    gather x2 -> x0, local copies, waits for them, and re-layouts: 18.2 us -> none  [the longest x1 14.7 us: local(): received.reshape(owners * slot_cap, page_width)]
  transfers between devices with their start and end apart: 4 -> 24, of which waited for: 3 -> 5; matrix products, arithmetic and copies ran while one was open for 16% -> 6% of each run, Pallas kernels for 0% -> 71%
where the time goes in v2:
time: 431 us; the launch traced here: 429 us
  Pallas kernels  316 us (73%)
  starting transfers between devices  38.6 us (9%)
  local copies, waits for them, and re-layouts  20 us (5%)
  waiting for transfers between devices  19.8 us (5%)
  other arithmetic  15.4 us (4%)
  between operations  14.6 us (3%)
  matrix products  4.35 us (1%)
    pallas_call x8, Pallas kernels, queue_chunk(): pl.pallas_call(functools.partial(queue_kernel, step, chunk, earliest), ou...  157 us
    pallas_call x1, Pallas kernels, join_pages(): pl.pallas_call(functools.partial(join_kernel, chunk), out_shape=(jax.Shap...  109 us
    pallas_call x3, Pallas kernels, attend(): pl.pallas_call(functools.partial(attend_kernel, shape, state is None, tai...  44.7 us
    ppermute x10, starting transfers between devices, local(): arrived.append(lax.ppermute(outgoing, ('head', 'seq'), stream_route))  30.7 us
    unnamed x60, local copies, waits for them, and re-layouts  14.3 us
    ppermute x10, waiting for transfers between devices, local(): arrived.append(lax.ppermute(outgoing, ('head', 'seq'), stream_route))  10.4 us
  transfers between devices with their start and end apart: 24, of which 5 were waited for; matrix products, arithmetic and copies ran while one was open for 6% of the time, Pallas kernels for 71%

profile of v2, /device:TPU:0, one launch (start us, length us, event | category | flops | bytes accessed | tf_op | source)
XLA Modules:
  0.0 428.7 jit_solution(16845231805084565004)
XLA Ops:
  7.2 0.8 copy-done.14
  8.0 1.7 copy-done.16
  9.7 0.7 copy-done.18
  10.4 5.4 %pick_pages.1 = (s32[2]{0:T(128)S(1)}, bf16[16,32,1152]{2,1,0:T(8,128)(2,1)S(1)}, bf16[1,8,32,1152]{3,2,1,0:T(8,128)(2,1)S(1)}) custom-call(s32[2,64]{1,0:T(2,128)S(1)} %bitcast.32, s32[2,64]{1,0:T(2,128)S(1)} %copy-done.18, bf16[32,36864]{1,0:T(8,128)(2,1)S(1)} %copy-done.16), custom_call_target="tpu_custom_call" | custom-call | flops 1000000000 | bytes 6000000 | tf_op jit(solution)/shard_map/pick_pages/pallas_call | solution.py:121
  15.8 1.0 copy-done.12
  17.3 2.9 collective-permute-start
  20.2 1.6 fusion
  21.9 0.6 dynamic_slice.12
  22.4 0.7 subtract_clamp_fusion
  23.1 0.7 add_convert_fusion.1
  23.8 0.6 dynamic_slice.13.refs_5_
  24.4 0.7 fusion.3
  25.4 8.2 %collective-permute-done = bf16[8,32,1152]{2,1,0:T(8,128)(2,1)S(1)} collective-permute-done((bf16[8,32,1152]{2,1,0:T(8,128)(2,1)S(1)}, bf16[8,32,1152]{2,1,0:T(8,128)(2,1)S(1)}, u32[]{:S(2)}, u32[]{:S(2)}) %collective-permute-start) | collective-permute-done | bytes 589856 | tf_op jit(solution)/shard_map/ppermute | solution.py:451
  33.6 0.6 fusion.7
  34.3 1.2 collective-permute-done.1.other_ref
  35.6 0.8 copy-done.21
  36.4 109.0 %join_pages.1 = (bf16[32,32,1152]{2,1,0:T(8,128)(2,1)}, bf16[8,32,1152]{2,1,0:T(8,128)(2,1)}, bf16[8,32,1152]{2,1,0:T(8,128)(2,1)}) custom-call(s32[2]{0:T(128)} %copy-done.13, bf16[16,32,1152]{2,1,0:T(8,128)(2,1)} %copy-done.12, bf16[1,8,32,1152]{3,2,1,0:T(8,128)(2,1)} %bitcast.37, bf16[1,8,32,1152]{3,2,1,0:T(8,128)(2,1)} %copy-done.21), custom_call_target="tpu_custom_call" | custom-call | bytes 6000000 | tf_op jit(solution)/shard_map/join_pages/pallas_call | solution.py:177
  145.4 3.8 collective-permute-start.2
  149.2 0.6 add_compare_fusion
  149.8 1.2 copy.22
  151.5 1.0 multiply_cosine_fusion
  152.4 3.5 collective-permute-start.3
  155.9 0.9 collective-permute-done.2.refs_0_.refs_3_
  156.9 0.8 copy-done.9
  157.7 19.6 %queue_chunk.8 = bf16[8,32,1152]{2,1,0:T(8,128)(2,1)} custom-call(s32[1]{0:T(128)} %bitcast.8.held_ref, bf16[32,32,1152]{2,1,0:T(8,128)(2,1)} %get-tuple-element.17.joined_ref.refs_2_, bf16[8,32,1152]{2,1,0:T(8,128)(2,1)} %copy-done.9), custom_call_target="tpu_custom_call" | custom-call | bytes 1000000 | tf_op jit(solution)/shard_map/queue_chunk/pallas_call | solution.py:220
  177.3 4.3 %collective-permute-start.4 = (bf16[8,32,1152]{2,1,0:T(8,128)(2,1)}, bf16[8,32,1152]{2,1,0:T(8,128)(2,1)S(1)}, u32[]{:S(2)}, u32[]{:S(2)}) collective-permute-start(bf16[8,32,1152]{2,1,0:T(8,128)(2,1)} %queue_chunk.8), channel_id=1, source_target_pairs={{0,4},{5,1},{4,8},{9,5},{8,12},{13,9},{2,6},{7,3},{6,10},{11,7},{1... | collective-permute-start | bytes 1769480 | tf_op jit(solution)/shard_map/ppermute | solution.py:497
  181.7 1.8 subtract_convert_fusion
  183.5 0.9 copy-done.1
  184.4 19.6 %queue_chunk.9 = bf16[8,32,1152]{2,1,0:T(8,128)(2,1)} custom-call(s32[1]{0:T(128)} %bitcast.8.held_ref, bf16[32,32,1152]{2,1,0:T(8,128)(2,1)} %get-tuple-element.17.joined_ref.refs_2_, bf16[8,32,1152]{2,1,0:T(8,128)(2,1)} %copy-done.9, bf16[8,32,1152]{2,1,0:T(8,128)(2,1)} %copy-done.1), custom_call_target="tpu_custom_call" | custom-call | bytes 1000000 | tf_op jit(solution)/shard_map/queue_chunk/pallas_call | solution.py:220
  204.0 3.5 collective-permute-start.8
  207.5 0.8 copy-done.3
  208.3 19.6 %queue_chunk.10 = bf16[8,32,1152]{2,1,0:T(8,128)(2,1)} custom-call(s32[1]{0:T(128)} %bitcast.8.held_ref, bf16[32,32,1152]{2,1,0:T(8,128)(2,1)} %get-tuple-element.17.joined_ref.refs_2_, bf16[8,32,1152]{2,1,0:T(8,128)(2,1)} %copy-done.9, bf16[8,32,1152]{2,1,0:T(8,128)(2,1)} %copy-done.1, bf16[8,32,1152]{2,1,0:T(8,128)(2,1)} %copy-done.3), custom_call_target="tpu_custom_call" | custom-call | bytes 1000000 | tf_op jit(solution)/shard_map/queue_chunk/pallas_call | solution.py:220
  227.9 3.5 collective-permute-start.9
  231.5 2.8 convolution_convert_fusion
  234.3 0.7 broadcast_in_dim.98
  235.1 1.8 broadcast_in_dim.99
  236.9 0.8 copy-done.5
  237.7 19.6 %queue_chunk.11 = bf16[8,32,1152]{2,1,0:T(8,128)(2,1)} custom-call(s32[1]{0:T(128)} %bitcast.8.held_ref, bf16[32,32,1152]{2,1,0:T(8,128)(2,1)} %get-tuple-element.17.joined_ref.refs_2_, bf16[8,32,1152]{2,1,0:T(8,128)(2,1)} %copy-done.1, bf16[8,32,1152]{2,1,0:T(8,128)(2,1)} %copy-done.3, bf16[8,32,1152]{2,1,0:T(8,128)(2,1)} %copy-done.5), custom_call_target="tpu_custom_call" | custom-call | bytes 1000000 | tf_op jit(solution)/shard_map/queue_chunk/pallas_call | solution.py:220
  257.3 2.7 collective-permute-start.10
  260.1 0.9 copy-done.7
  260.9 19.6 %queue_chunk.12 = bf16[8,32,1152]{2,1,0:T(8,128)(2,1)} custom-call(s32[1]{0:T(128)} %bitcast.8.held_ref, bf16[32,32,1152]{2,1,0:T(8,128)(2,1)} %get-tuple-element.17.joined_ref.refs_2_, bf16[8,32,1152]{2,1,0:T(8,128)(2,1)} %copy-done.3, bf16[8,32,1152]{2,1,0:T(8,128)(2,1)} %copy-done.5, bf16[8,32,1152]{2,1,0:T(8,128)(2,1)} %copy-done.7), custom_call_target="tpu_custom_call" | custom-call | bytes 1000000 | tf_op jit(solution)/shard_map/queue_chunk/pallas_call | solution.py:220
  280.5 2.3 collective-permute-start.11
  282.9 2.6 pad_maximum_fusion
  285.5 1.1 multiply_reduce_fusion
  286.6 1.2 multiply_subtract_fusion
  288.9 19.6 %queue_chunk.13 = bf16[8,32,1152]{2,1,0:T(8,128)(2,1)} custom-call(s32[1]{0:T(128)} %bitcast.8.held_ref, bf16[32,32,1152]{2,1,0:T(8,128)(2,1)} %get-tuple-element.17.joined_ref.refs_2_, bf16[8,32,1152]{2,1,0:T(8,128)(2,1)} %copy-done.5, bf16[8,32,1152]{2,1,0:T(8,128)(2,1)} %copy-done.7, ...), custom_call_target="tpu_custom_call" | custom-call | bytes 1000000 | tf_op jit(solution)/shard_map/queue_chunk/pallas_call | solution.py:220
  308.5 2.2 collective-permute-start.17
  310.7 1.0 multiply_multiply_fusion
  311.8 0.8 broadcast_select_fusion
  312.5 1.8 convert_element_type.48
  314.3 19.6 %queue_chunk.14 = bf16[8,32,1152]{2,1,0:T(8,128)(2,1)} custom-call(s32[1]{0:T(128)} %bitcast.8.held_ref, bf16[32,32,1152]{2,1,0:T(8,128)(2,1)} %get-tuple-element.17.joined_ref.refs_2_, bf16[8,32,1152]{2,1,0:T(8,128)(2,1)} %copy-done.7, bf16[8,32,1152]{2,1,0:T(8,128)(2,1)} %collective-permute-done.10.refs_7_.refs_2_.refs_1_.refs_0_, ...), custom_call_target="tpu_custom_call" | custom-call | bytes 1000000 | tf_op jit(solution)/shard_map/queue_chunk/pallas_call | solution.py:220
  334.0 19.6 %queue_chunk.15 = bf16[8,32,1152]{2,1,0:T(8,128)(2,1)} custom-call(s32[1]{0:T(128)} %bitcast.8.held_ref, bf16[32,32,1152]{2,1,0:T(8,128)(2,1)} %get-tuple-element.17.joined_ref.refs_2_, bf16[8,32,1152]{2,1,0:T(8,128)(2,1)} %collective-permute-done.10.refs_7_.refs_2_.refs_1_.refs_0_, bf16[8,32,1152]{2,1,0:T(8,128)(2,1)} %collective-permute-done.11.refs_8_.refs_2_.refs_1_, ...), custom_call_target="tpu_custom_call" | custom-call | bytes 1000000 | tf_op jit(solution)/shard_map/queue_chunk/pallas_call | solution.py:220
  354.2 3.0 collective-permute-start.18
  357.2 1.9 collective-permute-start.19
  359.3 1.9 broadcast_select_fusion.1
  361.6 3.3 collective-permute-done.18.refs_10_
  365.0 6.2 %collective-permute-done.19.refs_11_ = bf16[8,32,1152]{2,1,0:T(8,128)(2,1)S(1)} collective-permute-done((bf16[8,32,1152]{2,1,0:T(8,128)(2,1)}, bf16[8,32,1152]{2,1,0:T(8,128)(2,1)S(1)}, u32[]{:S(2)}, u32[]{:S(2)}) %collective-permute-start.19) | collective-permute-done | bytes 589856 | tf_op jit(solution)/shard_map/ppermute | solution.py:497
  371.4 1.1 copy-done.10
  372.4 1.3 copy-done.11
  373.8 20.7 %attend.3 = (f32[1024,512]{1,0:T(8,128)}, f32[1024,1]{1,0:T(8,128)S(1)}, f32[1024,1]{1,0:T(8,128)S(1)}) custom-call(s32[80]{0:T(128)S(1)} %pad_add_fusion.2.refs_0_, bf16[1024,576]{1,0:T(8,128)(2,1)S(1)} %bitcast.31, bf16[32,32,1152]{2,1,0:T(8,128)(2,1)} %get-tuple-element.17.joined_ref.refs_2_, bf16[8,32,1152]{2,1,0:T(8,128)(2,1)S(1)} %copy-done.10, ...), custom_call_target="tpu_custom_call" | custom-call | flops 5704253440 | bytes 10000000 | tf_op jit(solution)/shard_map/attend/pallas_call | solution.py:399
  394.5 2.4 collective-permute-start.16
  397.0 0.8 copy-done.26
  397.8 16.9 %attend.4 = (f32[1024,512]{1,0:T(8,128)}, f32[1024,1]{1,0:T(8,128)S(1)}, f32[1024,1]{1,0:T(8,128)S(1)}) custom-call(s32[64]{0:T(128)S(1)} %pad_add_fusion.1.refs_0_, bf16[1024,576]{1,0:T(8,128)(2,1)} %bitcast.29, f32[1024,512]{1,0:T(8,128)} %get-tuple-element.20.refs_2_, f32[1024,1]{1,0:T(8,128)S(1)} %get-tuple-element.21.refs_3_, ...), custom_call_target="tpu_custom_call" | custom-call | flops 4563402752 | bytes 10000000 | tf_op jit(solution)/shard_map/attend/pallas_call | solution.py:399
  414.8 7.1 %attend.5 = bf16[128,1024]{1,0:T(8,128)(2,1)} custom-call(s32[48]{0:T(128)S(1)} %pad_add_fusion.refs_0_, bf16[1024,576]{1,0:T(8,128)(2,1)} %bitcast.30, f32[1024,512]{1,0:T(8,128)} %get-tuple-element.23.refs_2_, f32[1024,1]{1,0:T(8,128)S(1)} %get-tuple-element.24.refs_3_, f32[1024,1]{1,0:T(8,128)S(1)} %get-tuple-element.25.refs_4_, s32[1]{0:T(128)} %dynamic_slice.13.refs_5_, ...), custom_call_target="tpu_custom_call" | custom-call | flops 3422552064 | bytes 10000000 | tf_op jit(solution)/shard_map/attend/pallas_call | solution.py:399
  (97 shorter events, 4.4 us)
Async XLA Ops:
  7.2 13.1 %copy-start = (bf16[1792,576]{0,1:T(8,128)(2,1)S(1)}, bf16[1792,576]{0,1:T(8,128)(2,1)}, u32[]{:S(2)}) copy-start(bf16[1792,576]{0,1:T(8,128)(2,1)} %param.13) | copy-start | bytes 6193156
  7.2 278.3 %all-reduce.2.cloned.1.call-start = ((), (), s32[]{:S(2)}) async-start(), calls=%async_computation | async-start | bytes 655360 | tf_op jit(solution)/shard_map/psum | solution.py:470
  7.2 0.8 copy-start.14
  8.0 1.7 copy-start.16
  9.7 0.7 copy-start.18
  10.4 9.8 %copy-start.22 = (bf16[1,128,1792]{2,1,0:T(8,128)(2,1)S(1)}, bf16[1,128,1792]{2,1,0:T(8,128)(2,1)}, u32[]{:S(2)}) copy-start(bf16[1,128,1792]{2,1,0:T(8,128)(2,1)} %param.12) | copy-start | bytes 1376260
  15.8 1.0 copy-start.12
  16.8 0.5 copy-start.13
  17.3 4.6 %copy-start.27 = (s32[2]{0:T(128)S(1)}, s32[2]{0:T(128)}, u32[]{:S(2)}) copy-start(s32[2]{0:T(128)} %param.20) | copy-start | bytes 28
  17.3 6.5 %copy-start.28 = (s32[2]{0:T(128)S(1)}, s32[2]{0:T(128)}, u32[]{:S(2)}) copy-start(s32[2]{0:T(128)} %param.21) | copy-start | bytes 28
  17.3 7.1 %copy-start.15 = (s32[2,64,1]{1,2,0:T(1,128)S(1)}, s32[2,64,1]{1,2,0:T(1,128)}, u32[]{:S(2)}) copy-start(s32[2,64,1]{1,2,0:T(1,128)} %param.18) | copy-start | bytes 1540
  17.3 16.3 %collective-permute-start = (bf16[8,32,1152]{2,1,0:T(8,128)(2,1)S(1)}, bf16[8,32,1152]{2,1,0:T(8,128)(2,1)S(1)}, u32[]{:S(2)}, u32[]{:S(2)}) collective-permute-start(bf16[8,32,1152]{2,1,0:T(8,128)(2,1)S(1)} %bitcast.33), channel_id=1, source_target_pairs={{0,2},{2,0},{1,3},{3,1},{4,6},{6,4},{5,7},{7,5},{8,10},{10,8},{9,1... | collective-permute-start | bytes 1769480 | tf_op jit(solution)/shard_map/ppermute | solution.py:451
  33.6 2.0 copy-start.20
  33.6 2.0 collective-permute-start.1
  35.6 0.8 copy-start.21
  145.4 11.4 %collective-permute-start.2 = (bf16[8,32,1152]{2,1,0:T(8,128)(2,1)}, bf16[8,32,1152]{2,1,0:T(8,128)(2,1)S(1)}, u32[]{:S(2)}, u32[]{:S(2)}) collective-permute-start(bf16[8,32,1152]{2,1,0:T(8,128)(2,1)} %get-tuple-element.18), channel_id=1, source_target_pairs={{0,4},{5,1},{4,8},{9,5},{8,12},{13,9},{2,6},{7,3},{6,10},{11,7},{1... | collective-permute-start | bytes 1769480 | tf_op jit(solution)/shard_map/ppermute | solution.py:497
  151.1 1.4 copy-start.19
  151.4 83.0 %copy-start.23 = (s32[192]{0:T(256)}, s32[192]{0:T(256)S(1)}, u32[]{:S(2)}) copy-start(s32[192]{0:T(256)S(1)} %select_reduce_fusion) | copy-start | bytes 2308
  152.4 31.1 %collective-permute-start.3 = (bf16[8,32,1152]{2,1,0:T(8,128)(2,1)}, bf16[8,32,1152]{2,1,0:T(8,128)(2,1)S(1)}, u32[]{:S(2)}, u32[]{:S(2)}) collective-permute-start(bf16[8,32,1152]{2,1,0:T(8,128)(2,1)} %get-tuple-element.19), channel_id=1, source_target_pairs={{0,4},{5,1},{4,8},{9,5},{8,12},{13,9},{2,6},{7,3},{6,10},{11,7},{1... | collective-permute-start | bytes 1769480 | tf_op jit(solution)/shard_map/ppermute | solution.py:497
  156.9 0.8 copy-start.9
  177.3 30.2 %collective-permute-start.4 = (bf16[8,32,1152]{2,1,0:T(8,128)(2,1)}, bf16[8,32,1152]{2,1,0:T(8,128)(2,1)S(1)}, u32[]{:S(2)}, u32[]{:S(2)}) collective-permute-start(bf16[8,32,1152]{2,1,0:T(8,128)(2,1)} %queue_chunk.8), channel_id=1, source_target_pairs={{0,4},{5,1},{4,8},{9,5},{8,12},{13,9},{2,6},{7,3},{6,10},{11,7},{1... | collective-permute-start | bytes 1769480 | tf_op jit(solution)/shard_map/ppermute | solution.py:497
  183.5 0.9 copy-start.1
  204.0 32.9 %collective-permute-start.8 = (bf16[8,32,1152]{2,1,0:T(8,128)(2,1)}, bf16[8,32,1152]{2,1,0:T(8,128)(2,1)S(1)}, u32[]{:S(2)}, u32[]{:S(2)}) collective-permute-start(bf16[8,32,1152]{2,1,0:T(8,128)(2,1)} %queue_chunk.9), channel_id=1, source_target_pairs={{0,4},{5,1},{4,8},{9,5},{8,12},{13,9},{2,6},{7,3},{6,10},{11,7},{1... | collective-permute-start | bytes 1769480 | tf_op jit(solution)/shard_map/ppermute | solution.py:497
  207.5 0.8 copy-start.3
  227.9 32.1 %collective-permute-start.9 = (bf16[8,32,1152]{2,1,0:T(8,128)(2,1)}, bf16[8,32,1152]{2,1,0:T(8,128)(2,1)S(1)}, u32[]{:S(2)}, u32[]{:S(2)}) collective-permute-start(bf16[8,32,1152]{2,1,0:T(8,128)(2,1)} %queue_chunk.10), channel_id=1, source_target_pairs={{0,4},{5,1},{4,8},{9,5},{8,12},{13,9},{2,6},{7,3},{6,10},{11,7},{1... | collective-permute-start | bytes 1769480 | tf_op jit(solution)/shard_map/ppermute | solution.py:497
  236.9 0.8 copy-start.5
  257.3 25.5 %slice-start = ((s32[192]{0:T(256)}), s32[56]{0:T(128)S(1)}, s32[]{:S(2)}) async-start(s32[192]{0:T(256)} %copy-done.23), calls=%async_computation.1 | async-start | bytes 1024 | tf_op jit(solution)/shard_map/slice | solution.py:516
  257.3 31.2 %collective-permute-start.10 = (bf16[8,32,1152]{2,1,0:T(8,128)(2,1)}, bf16[8,32,1152]{2,1,0:T(8,128)(2,1)}, u32[]{:S(2)}, u32[]{:S(2)}) collective-permute-start(bf16[8,32,1152]{2,1,0:T(8,128)(2,1)} %queue_chunk.11), channel_id=1, source_target_pairs={{0,4},{5,1},{4,8},{9,5},{8,12},{13,9},{2,6},{7,3},{6,10},{11,7},{1... | collective-permute-start | bytes 1769480 | tf_op jit(solution)/shard_map/ppermute | solution.py:497
  260.1 0.9 copy-start.7
  280.5 7.4 %copy-start.2 = (bf16[8,32,1152]{2,1,0:T(8,128)(2,1)S(1)}, bf16[8,32,1152]{2,1,0:T(8,128)(2,1)}, u32[]{:S(2)}) copy-start(bf16[8,32,1152]{2,1,0:T(8,128)(2,1)} %copy-done.1) | copy-start | bytes 1769476
  280.5 7.9 %copy-start.4 = (bf16[8,32,1152]{2,1,0:T(8,128)(2,1)S(1)}, bf16[8,32,1152]{2,1,0:T(8,128)(2,1)}, u32[]{:S(2)}) copy-start(bf16[8,32,1152]{2,1,0:T(8,128)(2,1)} %copy-done.3) | copy-start | bytes 1769476
  280.5 28.0 %collective-permute-start.11 = (bf16[8,32,1152]{2,1,0:T(8,128)(2,1)}, bf16[8,32,1152]{2,1,0:T(8,128)(2,1)}, u32[]{:S(2)}, u32[]{:S(2)}) collective-permute-start(bf16[8,32,1152]{2,1,0:T(8,128)(2,1)} %queue_chunk.12), channel_id=1, source_target_pairs={{0,4},{5,1},{4,8},{9,5},{8,12},{13,9},{2,6},{7,3},{6,10},{11,7},{1... | collective-permute-start | bytes 1769480 | tf_op jit(solution)/shard_map/ppermute | solution.py:497
  287.8 22.9 %copy-start.24 = (f32[512]{0:T(512)S(1)}, f32[512]{0:T(512)}, u32[]{:S(2)}) copy-start(f32[512]{0:T(512)} %param.14) | copy-start | bytes 6148
  287.8 65.8 %collective-permute-start.5 = (bf16[8,32,1152]{2,1,0:T(8,128)(2,1)}, bf16[8,32,1152]{2,1,0:T(8,128)(2,1)}, u32[]{:S(2)}, u32[]{:S(2)}) collective-permute-start(bf16[8,32,1152]{2,1,0:T(8,128)(2,1)} %copy-done.9), channel_id=1, source_target_pairs={{0,1},{1,0},{2,3},{3,2},{4,5},{5,4},{6,7},{7,6},{8,9},{9,8},{10,11... | collective-permute-start | bytes 1769480 | tf_op jit(solution)/shard_map/ppermute | solution.py:498
  287.9 66.3 %collective-permute-start.6 = (bf16[8,32,1152]{2,1,0:T(8,128)(2,1)S(1)}, bf16[8,32,1152]{2,1,0:T(8,128)(2,1)}, u32[]{:S(2)}, u32[]{:S(2)}) collective-permute-start(bf16[8,32,1152]{2,1,0:T(8,128)(2,1)S(1)} %copy-done.2), channel_id=1, source_target_pairs={{0,1},{1,0},{2,3},{3,2},{4,5},{5,4},{6,7},{7,6},{8,9},{9,8},{10,11... | collective-permute-start | bytes 1769480 | tf_op jit(solution)/shard_map/ppermute | solution.py:498
  288.4 68.8 %collective-permute-start.7 = (bf16[8,32,1152]{2,1,0:T(8,128)(2,1)S(1)}, bf16[8,32,1152]{2,1,0:T(8,128)(2,1)}, u32[]{:S(2)}, u32[]{:S(2)}) collective-permute-start(bf16[8,32,1152]{2,1,0:T(8,128)(2,1)S(1)} %copy-done.4), channel_id=1, source_target_pairs={{0,1},{1,0},{2,3},{3,2},{4,5},{5,4},{6,7},{7,6},{8,9},{9,8},{10,11... | collective-permute-start | bytes 1769480 | tf_op jit(solution)/shard_map/ppermute | solution.py:498
  288.5 70.7 %collective-permute-start.12 = (bf16[8,32,1152]{2,1,0:T(8,128)(2,1)}, bf16[8,32,1152]{2,1,0:T(8,128)(2,1)}, u32[]{:S(2)}, u32[]{:S(2)}) collective-permute-start(bf16[8,32,1152]{2,1,0:T(8,128)(2,1)} %copy-done.5), channel_id=1, source_target_pairs={{0,1},{1,0},{2,3},{3,2},{4,5},{5,4},{6,7},{7,6},{8,9},{9,8},{10,11... | collective-permute-start | bytes 1769480 | tf_op jit(solution)/shard_map/ppermute | solution.py:498
  308.5 25.4 %collective-permute-start.17 = (bf16[8,32,1152]{2,1,0:T(8,128)(2,1)}, bf16[8,32,1152]{2,1,0:T(8,128)(2,1)}, u32[]{:S(2)}, u32[]{:S(2)}) collective-permute-start(bf16[8,32,1152]{2,1,0:T(8,128)(2,1)} %queue_chunk.13), channel_id=1, source_target_pairs={{0,4},{5,1},{4,8},{9,5},{8,12},{13,9},{2,6},{7,3},{6,10},{11,7},{1... | collective-permute-start | bytes 1769480 | tf_op jit(solution)/shard_map/ppermute | solution.py:497
  333.9 27.2 %collective-permute-start.13 = (bf16[8,32,1152]{2,1,0:T(8,128)(2,1)}, bf16[8,32,1152]{2,1,0:T(8,128)(2,1)}, u32[]{:S(2)}, u32[]{:S(2)}) collective-permute-start(bf16[8,32,1152]{2,1,0:T(8,128)(2,1)} %copy-done.7), channel_id=1, source_target_pairs={{0,1},{1,0},{2,3},{3,2},{4,5},{5,4},{6,7},{7,6},{8,9},{9,8},{10,11... | collective-permute-start | bytes 1769480 | tf_op jit(solution)/shard_map/ppermute | solution.py:498
  353.6 40.9 %collective-permute-start.14 = (bf16[8,32,1152]{2,1,0:T(8,128)(2,1)}, bf16[8,32,1152]{2,1,0:T(8,128)(2,1)S(1)}, u32[]{:S(2)}, u32[]{:S(2)}) collective-permute-start(bf16[8,32,1152]{2,1,0:T(8,128)(2,1)} %collective-permute-done.10.refs_7_.refs_2_.refs_1_.refs_0_), channel_id=1, source_target_pairs={{0,1},{1,0},{2,3},{3,2},{4,5},{5,4},{6,7},{7,6},{8,9},{9,8},{10,11... | collective-permute-start | bytes 1769480 | tf_op jit(solution)/shard_map/ppermute | solution.py:498
  354.2 10.7 %collective-permute-start.18 = (bf16[8,32,1152]{2,1,0:T(8,128)(2,1)}, bf16[8,32,1152]{2,1,0:T(8,128)(2,1)S(1)}, u32[]{:S(2)}, u32[]{:S(2)}) collective-permute-start(bf16[8,32,1152]{2,1,0:T(8,128)(2,1)} %queue_chunk.14), channel_id=1, source_target_pairs={{0,4},{5,1},{4,8},{9,5},{8,12},{13,9},{2,6},{7,3},{6,10},{11,7},{1... | collective-permute-start | bytes 1769480 | tf_op jit(solution)/shard_map/ppermute | solution.py:497
  357.2 14.0 %collective-permute-start.19 = (bf16[8,32,1152]{2,1,0:T(8,128)(2,1)}, bf16[8,32,1152]{2,1,0:T(8,128)(2,1)S(1)}, u32[]{:S(2)}, u32[]{:S(2)}) collective-permute-start(bf16[8,32,1152]{2,1,0:T(8,128)(2,1)} %queue_chunk.15), channel_id=1, source_target_pairs={{0,4},{5,1},{4,8},{9,5},{8,12},{13,9},{2,6},{7,3},{6,10},{11,7},{1... | collective-permute-start | bytes 1769480 | tf_op jit(solution)/shard_map/ppermute | solution.py:497
  359.2 37.8 %collective-permute-start.15 = (bf16[8,32,1152]{2,1,0:T(8,128)(2,1)}, bf16[8,32,1152]{2,1,0:T(8,128)(2,1)S(1)}, u32[]{:S(2)}, u32[]{:S(2)}) collective-permute-start(bf16[8,32,1152]{2,1,0:T(8,128)(2,1)} %collective-permute-done.11.refs_8_.refs_2_.refs_1_), channel_id=1, source_target_pairs={{0,1},{1,0},{2,3},{3,2},{4,5},{5,4},{6,7},{7,6},{8,9},{9,8},{10,11... | collective-permute-start | bytes 1769480 | tf_op jit(solution)/shard_map/ppermute | solution.py:498
  361.1 53.6 %collective-permute-start.20 = (bf16[8,32,1152]{2,1,0:T(8,128)(2,1)}, bf16[8,32,1152]{2,1,0:T(8,128)(2,1)S(1)}, u32[]{:S(2)}, u32[]{:S(2)}) collective-permute-start(bf16[8,32,1152]{2,1,0:T(8,128)(2,1)} %collective-permute-done.17.refs_2_.refs_9_), channel_id=1, source_target_pairs={{0,1},{1,0},{2,3},{3,2},{4,5},{5,4},{6,7},{7,6},{8,9},{9,8},{10,11... | collective-permute-start | bytes 1769480 | tf_op jit(solution)/shard_map/ppermute | solution.py:498
  364.9 49.9 %collective-permute-start.21 = (bf16[8,32,1152]{2,1,0:T(8,128)(2,1)S(1)}, bf16[8,32,1152]{2,1,0:T(8,128)(2,1)S(1)}, u32[]{:S(2)}, u32[]{:S(2)}) collective-permute-start(bf16[8,32,1152]{2,1,0:T(8,128)(2,1)S(1)} %collective-permute-done.18.refs_10_), channel_id=1, source_target_pairs={{0,1},{1,0},{2,3},{3,2},{4,5},{5,4},{6,7},{7,6},{8,9},{9,8},{10,11... | collective-permute-start | bytes 1769480 | tf_op jit(solution)/shard_map/ppermute | solution.py:498
  371.2 43.6 %collective-permute-start.22 = (bf16[8,32,1152]{2,1,0:T(8,128)(2,1)S(1)}, bf16[8,32,1152]{2,1,0:T(8,128)(2,1)S(1)}, u32[]{:S(2)}, u32[]{:S(2)}) collective-permute-start(bf16[8,32,1152]{2,1,0:T(8,128)(2,1)S(1)} %collective-permute-done.19.refs_11_), channel_id=1, source_target_pairs={{0,1},{1,0},{2,3},{3,2},{4,5},{5,4},{6,7},{7,6},{8,9},{9,8},{10,11... | collective-permute-start | bytes 1769480 | tf_op jit(solution)/shard_map/ppermute | solution.py:498
  371.4 1.1 copy-start.10
  372.4 1.3 copy-start.11
  373.7 24.1 %copy-start.6 = (bf16[8,32,1152]{2,1,0:T(8,128)(2,1)S(1)}, bf16[8,32,1152]{2,1,0:T(8,128)(2,1)}, u32[]{:S(2)}) copy-start(bf16[8,32,1152]{2,1,0:T(8,128)(2,1)} %copy-done.5) | copy-start | bytes 1769476
  373.7 24.1 %copy-start.8 = (bf16[8,32,1152]{2,1,0:T(8,128)(2,1)S(1)}, bf16[8,32,1152]{2,1,0:T(8,128)(2,1)}, u32[]{:S(2)}) copy-start(bf16[8,32,1152]{2,1,0:T(8,128)(2,1)} %copy-done.7) | copy-start | bytes 1769476
  394.5 2.5 copy-start.25
  394.5 20.2 %collective-permute-start.16 = (bf16[128,576]{1,0:T(8,128)(2,1)S(1)}, bf16[128,576]{1,0:T(8,128)(2,1)S(1)}, u32[]{:S(2)}, u32[]{:S(2)}) collective-permute-start(bf16[128,576]{1,0:T(8,128)(2,1)S(1)} %get-tuple-element.30.refs_7_), channel_id=1, source_target_pairs={{0,1},{2,3},{4,5},{6,7},{8,9},{10,11},{12,13},{14,15},{16,17},{18,... | collective-permute-start | bytes 442376 | tf_op jit(solution)/shard_map/ppermute | solution.py:18
  397.0 0.8 copy-start.26
  397.8 17.0 %copy-start.17 = (bf16[8,512,128]{2,1,0:T(8,128)(2,1)S(1)}, bf16[8,512,128]{2,1,0:T(8,128)(2,1)}, u32[]{:S(2)}) copy-start(bf16[8,512,128]{2,1,0:T(8,128)(2,1)} %refs_8_.1) | copy-start | bytes 3145732
Sparse Core Ops, SparseCore 0:
  21.9 36.5 all-reduce.1

commit v3 on v2

--- a/solution.py
+++ b/solution.py
@@ -182,8 +182,9 @@
             jax.ShapeDtypeStruct((chunk, *page), jnp.bfloat16),
         ),
         in_specs=[smem_spec(), any_spec(), any_spec(), any_spec()],
-        out_specs=(any_spec(), any_spec(), any_spec()),
+        out_specs=(vmem_spec(), vmem_spec(), vmem_spec()),
         scratch_shapes=[pltpu.SemaphoreType.DMA((3,))],
+        compiler_params=pltpu.CompilerParams(vmem_limit_bytes=VMEM_LIMIT),
         cost_estimate=pl.CostEstimate(flops=0, bytes_accessed=6 * 10**6, transcendentals=0),
         name="join_pages",
     )(counts, own, mine, other)
@@ -221,8 +222,9 @@
         functools.partial(queue_kernel, step, chunk, earliest),
         out_shape=jax.ShapeDtypeStruct((chunk, *joined.shape[1:]), jnp.bfloat16),
         in_specs=[smem_spec()] + [any_spec()] * (1 + len(sources)),
-        out_specs=any_spec(),
+        out_specs=vmem_spec(),
         scratch_shapes=[pltpu.SemaphoreType.DMA],
+        compiler_params=pltpu.CompilerParams(vmem_limit_bytes=VMEM_LIMIT),
         cost_estimate=pl.CostEstimate(flops=0, bytes_accessed=10**6, transcendentals=0),
         name="queue_chunk",
     )(held, joined, *sources)

time: 431 us -> 194 us (0.45)
  the two profiles are of different devices: /device:TPU:0 before, /device:TPU:10 now
where the time goes in v3:
time: 194 us; the launch traced here: 193 us
  Pallas kernels  73.9 us (38%)
  starting transfers between devices  36.1 us (19%)
  waiting for transfers between devices  33.3 us (17%)
  local copies, waits for them, and re-layouts  21 us (11%)
  between operations  14.7 us (8%)
  other arithmetic  10.8 us (6%)
  matrix products  3.02 us (2%)
    pallas_call x3, Pallas kernels, attend(): pl.pallas_call(functools.partial(attend_kernel, shape, state is None, tai...  44.9 us
    ppermute x10, starting transfers between devices, local(): arrived.append(lax.ppermute(outgoing, ('head', 'seq'), stream_route))  30.9 us
    ppermute x10, waiting for transfers between devices, local(): arrived.append(lax.ppermute(outgoing, ('head', 'seq'), stream_route))  22.1 us
    pallas_call x8, Pallas kernels, queue_chunk(): pl.pallas_call(functools.partial(queue_kernel, step, chunk, earliest), ou...  18.1 us
    unnamed x64, local copies, waits for them, and re-layouts  15.2 us
    ppermute x1, waiting for transfers between devices, local(): lax.ppermute(foreign[s - 1], 'req', [(i, (i + s) % n_req) for i in range(...  9.66 us
    pallas_call x1, Pallas kernels, join_pages(): pl.pallas_call(functools.partial(join_kernel, chunk), out_shape=(jax.Shap...  5.81 us
    pallas_call x1, Pallas kernels, pick_pages(): pl.pallas_call(functools.partial(pick_kernel, cap), out_shape=(jax.ShapeD...  5.1 us
  transfers between devices with their start and end apart: 24, of which 8 were waited for; matrix products, arithmetic and copies ran while one was open for 11% of the time, Pallas kernels for 32%

profile of v3, /device:TPU:10, one launch (start us, length us, event | category | flops | bytes accessed | tf_op | source)
XLA Modules:
  0.0 192.9 jit_solution(14553889411200818072)
XLA Ops:
  7.2 0.8 copy-done.10
  8.0 1.7 copy-done.12
  9.7 0.7 copy-done.15
  10.4 5.1 %pick_pages.1 = (s32[2]{0:T(128)S(1)}, bf16[16,32,1152]{2,1,0:T(8,128)(2,1)S(1)}, bf16[1,8,32,1152]{3,2,1,0:T(8,128)(2,1)}) custom-call(s32[2,64]{1,0:T(2,128)S(1)} %bitcast.32, s32[2,64]{1,0:T(2,128)S(1)} %copy-done.15, bf16[32,36864]{1,0:T(8,128)(2,1)S(1)} %copy-done.12), custom_call_target="tpu_custom_call" | custom-call | flops 1000000000 | bytes 6000000 | tf_op jit(solution)/shard_map/pick_pages/pallas_call | solution.py:121
  15.5 0.6 collective-permute-start
  16.1 1.6 fusion
  17.8 0.6 dynamic_slice.12
  18.3 0.7 subtract_clamp_fusion
  19.0 0.7 add_convert_fusion.1
  19.7 0.7 dynamic_slice.13.refs_5_
  20.3 0.7 fusion.3
  21.3 9.7 %collective-permute-done = bf16[8,32,1152]{2,1,0:T(8,128)(2,1)} collective-permute-done((bf16[8,32,1152]{2,1,0:T(8,128)(2,1)}, bf16[8,32,1152]{2,1,0:T(8,128)(2,1)}, u32[]{:S(2)}, u32[]{:S(2)}) %collective-permute-start) | collective-permute-done | bytes 589856 | tf_op jit(solution)/shard_map/ppermute | solution.py:453
  31.0 0.7 fusion.7
  31.8 1.5 collective-permute-done.1.other_ref
  33.3 5.8 %join_pages.1 = (bf16[32,32,1152]{2,1,0:T(8,128)(2,1)S(1)}, bf16[8,32,1152]{2,1,0:T(8,128)(2,1)}, bf16[8,32,1152]{2,1,0:T(8,128)(2,1)S(1)}) custom-call(s32[2]{0:T(128)S(1)} %get-tuple-element.14.count_ref, bf16[16,32,1152]{2,1,0:T(8,128)(2,1)S(1)} %get-tuple-element.15.own_ref, bf16[1,8,32,1152]{3,2,1,0:T(8,128)(2,1)} %bitcast.7.mine_ref, ...), custom_call_target="tpu_custom_call" | custom-call | bytes 6000000 | tf_op jit(solution)/shard_map/join_pages/pallas_call | solution.py:177
  39.2 1.4 copy-done.1
  40.6 0.8 copy-done.14
  41.4 2.8 %collective-permute-start.2 = (bf16[8,32,1152]{2,1,0:T(8,128)(2,1)}, bf16[8,32,1152]{2,1,0:T(8,128)(2,1)S(1)}, u32[]{:S(2)}, u32[]{:S(2)}) collective-permute-start(bf16[8,32,1152]{2,1,0:T(8,128)(2,1)} %get-tuple-element.18), channel_id=1, source_target_pairs={{0,4},{5,1},{4,8},{9,5},{8,12},{13,9},{2,6},{7,3},{6,10},{11,7},{1... | collective-permute-start | bytes 1769480 | tf_op jit(solution)/shard_map/ppermute | solution.py:499
  44.2 0.7 add_compare_fusion
  44.9 1.2 copy.22
  46.9 3.8 %collective-permute-start.3 = (bf16[8,32,1152]{2,1,0:T(8,128)(2,1)}, bf16[8,32,1152]{2,1,0:T(8,128)(2,1)S(1)}, u32[]{:S(2)}, u32[]{:S(2)}) collective-permute-start(bf16[8,32,1152]{2,1,0:T(8,128)(2,1)} %copy-done.14), channel_id=1, source_target_pairs={{0,4},{5,1},{4,8},{9,5},{8,12},{13,9},{2,6},{7,3},{6,10},{11,7},{1... | collective-permute-start | bytes 1769480 | tf_op jit(solution)/shard_map/ppermute | solution.py:499
  50.8 6.0 %collective-permute-done.2.refs_0_.refs_3_ = bf16[8,32,1152]{2,1,0:T(8,128)(2,1)S(1)} collective-permute-done((bf16[8,32,1152]{2,1,0:T(8,128)(2,1)}, bf16[8,32,1152]{2,1,0:T(8,128)(2,1)S(1)}, u32[]{:S(2)}, u32[]{:S(2)}) %collective-permute-start.2) | collective-permute-done | bytes 589856 | tf_op jit(solution)/shard_map/ppermute | solution.py:499
  56.8 1.7 copy-done.2
  58.5 1.5 queue_chunk.8
  60.0 0.8 copy-done.6
  60.8 2.8 %collective-permute-start.4 = (bf16[8,32,1152]{2,1,0:T(8,128)(2,1)S(1)}, bf16[8,32,1152]{2,1,0:T(8,128)(2,1)S(1)}, u32[]{:S(2)}, u32[]{:S(2)}) collective-permute-start(bf16[8,32,1152]{2,1,0:T(8,128)(2,1)S(1)} %queue_chunk.8), channel_id=1, source_target_pairs={{0,4},{5,1},{4,8},{9,5},{8,12},{13,9},{2,6},{7,3},{6,10},{11,7},{1... | collective-permute-start | bytes 1769480 | tf_op jit(solution)/shard_map/ppermute | solution.py:499
  63.8 0.9 subtract_convert_fusion
  64.7 2.4 %queue_chunk.9 = bf16[8,32,1152]{2,1,0:T(8,128)(2,1)} custom-call(s32[1]{0:T(128)} %bitcast.8.held_ref, bf16[32,32,1152]{2,1,0:T(8,128)(2,1)S(1)} %copy-done.2, bf16[8,32,1152]{2,1,0:T(8,128)(2,1)S(1)} %copy-done.7, bf16[8,32,1152]{2,1,0:T(8,128)(2,1)S(1)} %collective-permute-done.3.refs_4_.refs_1_.refs_0_), custom_call_target="tpu_custom_call" | custom-call | bytes 1000000 | tf_op jit(solution)/shard_map/queue_chunk/pallas_call | solution.py:221
  67.2 3.8 %collective-permute-start.8 = (bf16[8,32,1152]{2,1,0:T(8,128)(2,1)}, bf16[8,32,1152]{2,1,0:T(8,128)(2,1)}, u32[]{:S(2)}, u32[]{:S(2)}) collective-permute-start(bf16[8,32,1152]{2,1,0:T(8,128)(2,1)} %queue_chunk.9), channel_id=1, source_target_pairs={{0,4},{5,1},{4,8},{9,5},{8,12},{13,9},{2,6},{7,3},{6,10},{11,7},{1... | collective-permute-start | bytes 1769480 | tf_op jit(solution)/shard_map/ppermute | solution.py:499
  70.9 1.7 collective-permute-done.4.refs_5_.refs_2_.refs_1_.refs_0_
  72.6 2.5 %queue_chunk.10 = bf16[8,32,1152]{2,1,0:T(8,128)(2,1)} custom-call(s32[1]{0:T(128)} %bitcast.8.held_ref, bf16[32,32,1152]{2,1,0:T(8,128)(2,1)S(1)} %copy-done.2, bf16[8,32,1152]{2,1,0:T(8,128)(2,1)S(1)} %copy-done.7, bf16[8,32,1152]{2,1,0:T(8,128)(2,1)S(1)} %collective-permute-done.3.refs_4_.refs_1_.refs_0_, ...), custom_call_target="tpu_custom_call" | custom-call | bytes 1000000 | tf_op jit(solution)/shard_map/queue_chunk/pallas_call | solution.py:221
  75.1 2.8 %collective-permute-start.9 = (bf16[8,32,1152]{2,1,0:T(8,128)(2,1)}, bf16[8,32,1152]{2,1,0:T(8,128)(2,1)}, u32[]{:S(2)}, u32[]{:S(2)}) collective-permute-start(bf16[8,32,1152]{2,1,0:T(8,128)(2,1)} %queue_chunk.10), channel_id=1, source_target_pairs={{0,4},{5,1},{4,8},{9,5},{8,12},{13,9},{2,6},{7,3},{6,10},{11,7},{1... | collective-permute-start | bytes 1769480 | tf_op jit(solution)/shard_map/ppermute | solution.py:499
  78.0 1.5 convolution_convert_fusion
  79.6 0.7 broadcast_in_dim.98
  80.3 1.8 broadcast_in_dim.99
  82.1 1.7 copy-done.3
  83.8 2.8 %queue_chunk.11 = bf16[8,32,1152]{2,1,0:T(8,128)(2,1)} custom-call(s32[1]{0:T(128)} %bitcast.8.held_ref, bf16[32,32,1152]{2,1,0:T(8,128)(2,1)S(1)} %copy-done.3, bf16[8,32,1152]{2,1,0:T(8,128)(2,1)S(1)} %collective-permute-done.3.refs_4_.refs_1_.refs_0_, bf16[8,32,1152]{2,1,0:T(8,128)(2,1)S(1)} %collective-permute-done.4.refs_5_.refs_2_.refs_1_.refs_0_, ...), custom_call_target="tpu_custom_call" | custom-call | bytes 1000000 | tf_op jit(solution)/shard_map/queue_chunk/pallas_call | solution.py:221
  86.6 3.7 %collective-permute-start.10 = (bf16[8,32,1152]{2,1,0:T(8,128)(2,1)}, bf16[8,32,1152]{2,1,0:T(8,128)(2,1)}, u32[]{:S(2)}, u32[]{:S(2)}) collective-permute-start(bf16[8,32,1152]{2,1,0:T(8,128)(2,1)} %queue_chunk.11), channel_id=1, source_target_pairs={{0,4},{5,1},{4,8},{9,5},{8,12},{13,9},{2,6},{7,3},{6,10},{11,7},{1... | collective-permute-start | bytes 1769480 | tf_op jit(solution)/shard_map/ppermute | solution.py:499
  90.3 2.6 %queue_chunk.12 = bf16[8,32,1152]{2,1,0:T(8,128)(2,1)} custom-call(s32[1]{0:T(128)} %bitcast.8.held_ref, bf16[32,32,1152]{2,1,0:T(8,128)(2,1)S(1)} %copy-done.3, bf16[8,32,1152]{2,1,0:T(8,128)(2,1)S(1)} %collective-permute-done.4.refs_5_.refs_2_.refs_1_.refs_0_, bf16[8,32,1152]{2,1,0:T(8,128)(2,1)} %collective-permute-done.8.refs_2_.refs_1_.refs_5_.refs_0_, ...), custom_call_target="tpu_custom_call" | custom-call | bytes 1000000 | tf_op jit(solution)/shard_map/queue_chunk/pallas_call | solution.py:221
  93.0 1.9 collective-permute-start.11
  95.0 1.3 pad_maximum_fusion
  96.3 1.1 multiply_reduce_fusion
  97.4 1.2 multiply_subtract_fusion
  99.8 1.7 copy-done.4
  101.4 2.6 %queue_chunk.13 = bf16[8,32,1152]{2,1,0:T(8,128)(2,1)} custom-call(s32[1]{0:T(128)} %bitcast.8.held_ref, bf16[32,32,1152]{2,1,0:T(8,128)(2,1)S(1)} %copy-done.4, bf16[8,32,1152]{2,1,0:T(8,128)(2,1)} %collective-permute-done.8.refs_2_.refs_1_.refs_5_.refs_0_, bf16[8,32,1152]{2,1,0:T(8,128)(2,1)} %collective-permute-done.9.refs_2_.refs_6_.refs_1_.refs_0_, ...), custom_call_target="tpu_custom_call" | custom-call | bytes 1000000 | tf_op jit(solution)/shard_map/queue_chunk/pallas_call | solution.py:221
  104.1 1.1 collective-permute-done.11.refs_8_.refs_2_.refs_1_
  105.2 3.5 %collective-permute-start.17 = (bf16[8,32,1152]{2,1,0:T(8,128)(2,1)}, bf16[8,32,1152]{2,1,0:T(8,128)(2,1)}, u32[]{:S(2)}, u32[]{:S(2)}) collective-permute-start(bf16[8,32,1152]{2,1,0:T(8,128)(2,1)} %queue_chunk.13), channel_id=1, source_target_pairs={{0,4},{5,1},{4,8},{9,5},{8,12},{13,9},{2,6},{7,3},{6,10},{11,7},{1... | collective-permute-start | bytes 1769480 | tf_op jit(solution)/shard_map/ppermute | solution.py:499
  108.8 0.8 broadcast_select_fusion
  109.6 1.8 convert_element_type.48
  111.4 1.7 copy-done.5
  113.0 1.8 queue_chunk.14
  114.9 2.4 %collective-permute-done.17.refs_2_.refs_9_ = bf16[8,32,1152]{2,1,0:T(8,128)(2,1)} collective-permute-done((bf16[8,32,1152]{2,1,0:T(8,128)(2,1)}, bf16[8,32,1152]{2,1,0:T(8,128)(2,1)}, u32[]{:S(2)}, u32[]{:S(2)}) %collective-permute-start.17) | collective-permute-done | bytes 589856 | tf_op jit(solution)/shard_map/ppermute | solution.py:499
  117.3 1.8 queue_chunk.15
  119.1 0.6 collective-permute-start.14
  119.7 3.5 %collective-permute-start.18 = (bf16[8,32,1152]{2,1,0:T(8,128)(2,1)S(1)}, bf16[8,32,1152]{2,1,0:T(8,128)(2,1)S(1)}, u32[]{:S(2)}, u32[]{:S(2)}) collective-permute-start(bf16[8,32,1152]{2,1,0:T(8,128)(2,1)S(1)} %queue_chunk.14), channel_id=1, source_target_pairs={{0,4},{5,1},{4,8},{9,5},{8,12},{13,9},{2,6},{7,3},{6,10},{11,7},{1... | collective-permute-start | bytes 1769480 | tf_op jit(solution)/shard_map/ppermute | solution.py:499
  123.2 2.1 %collective-permute-start.19 = (bf16[8,32,1152]{2,1,0:T(8,128)(2,1)S(1)}, bf16[8,32,1152]{2,1,0:T(8,128)(2,1)S(1)}, u32[]{:S(2)}, u32[]{:S(2)}) collective-permute-start(bf16[8,32,1152]{2,1,0:T(8,128)(2,1)S(1)} %queue_chunk.15), channel_id=1, source_target_pairs={{0,4},{5,1},{4,8},{9,5},{8,12},{13,9},{2,6},{7,3},{6,10},{11,7},{1... | collective-permute-start | bytes 1769480 | tf_op jit(solution)/shard_map/ppermute | solution.py:499
  125.4 0.9 broadcast_select_fusion.1
  126.8 4.6 %collective-permute-done.18.refs_10_ = bf16[8,32,1152]{2,1,0:T(8,128)(2,1)S(1)} collective-permute-done((bf16[8,32,1152]{2,1,0:T(8,128)(2,1)S(1)}, bf16[8,32,1152]{2,1,0:T(8,128)(2,1)S(1)}, u32[]{:S(2)}, u32[]{:S(2)}) %collective-permute-start.18) | collective-permute-done | bytes 589856 | tf_op jit(solution)/shard_map/ppermute | solution.py:499
  131.4 6.3 %collective-permute-done.19.refs_11_ = bf16[8,32,1152]{2,1,0:T(8,128)(2,1)S(1)} collective-permute-done((bf16[8,32,1152]{2,1,0:T(8,128)(2,1)S(1)}, bf16[8,32,1152]{2,1,0:T(8,128)(2,1)S(1)}, u32[]{:S(2)}, u32[]{:S(2)}) %collective-permute-start.19) | collective-permute-done | bytes 589856 | tf_op jit(solution)/shard_map/ppermute | solution.py:499
  137.8 26.6 %attend.3 = (f32[1024,512]{1,0:T(8,128)}, f32[1024,1]{1,0:T(8,128)S(1)}, f32[1024,1]{1,0:T(8,128)S(1)}) custom-call(s32[80]{0:T(128)S(1)} %pad_add_fusion.2.refs_0_, bf16[1024,576]{1,0:T(8,128)(2,1)S(1)} %bitcast.31, bf16[32,32,1152]{2,1,0:T(8,128)(2,1)} %copy-done.1, bf16[8,32,1152]{2,1,0:T(8,128)(2,1)S(1)} %copy-done.8, ...), custom_call_target="tpu_custom_call" | custom-call | flops 5704253440 | bytes 10000000 | tf_op jit(solution)/shard_map/attend/pallas_call | solution.py:401
  164.3 2.4 %collective-permute-start.16 = (bf16[128,576]{1,0:T(8,128)(2,1)S(1)}, bf16[128,576]{1,0:T(8,128)(2,1)S(1)}, u32[]{:S(2)}, u32[]{:S(2)}) collective-permute-start(bf16[128,576]{1,0:T(8,128)(2,1)S(1)} %get-tuple-element.30.refs_7_), channel_id=1, source_target_pairs={{0,1},{2,3},{4,5},{6,7},{8,9},{10,11},{12,13},{14,15},{16,17},{18,... | collective-permute-start | bytes 442376 | tf_op jit(solution)/shard_map/ppermute | solution.py:18
  166.8 0.8 copy-done.28
  167.6 11.2 %attend.4 = (f32[1024,512]{1,0:T(8,128)}, f32[1024,1]{1,0:T(8,128)S(1)}, f32[1024,1]{1,0:T(8,128)S(1)}) custom-call(s32[64]{0:T(128)S(1)} %pad_add_fusion.1.refs_0_, bf16[1024,576]{1,0:T(8,128)(2,1)} %bitcast.29, f32[1024,512]{1,0:T(8,128)} %get-tuple-element.20.refs_2_, f32[1024,1]{1,0:T(8,128)S(1)} %get-tuple-element.21.refs_3_, ...), custom_call_target="tpu_custom_call" | custom-call | flops 4563402752 | bytes 10000000 | tf_op jit(solution)/shard_map/attend/pallas_call | solution.py:401
  178.9 7.1 %attend.5 = bf16[128,1024]{1,0:T(8,128)(2,1)} custom-call(s32[48]{0:T(128)S(1)} %pad_add_fusion.refs_0_, bf16[1024,576]{1,0:T(8,128)(2,1)} %bitcast.30, f32[1024,512]{1,0:T(8,128)} %get-tuple-element.23.refs_2_, f32[1024,1]{1,0:T(8,128)S(1)} %get-tuple-element.24.refs_3_, f32[1024,1]{1,0:T(8,128)S(1)} %get-tuple-element.25.refs_4_, s32[1]{0:T(128)} %dynamic_slice.13.refs_5_, ...), custom_call_target="tpu_custom_call" | custom-call | flops 3422552064 | bytes 10000000 | tf_op jit(solution)/shard_map/attend/pallas_call | solution.py:401
  (101 shorter events, 3.4 us)
Async XLA Ops:
  7.2 9.0 %copy-start = (bf16[1792,576]{0,1:T(8,128)(2,1)S(1)}, bf16[1792,576]{0,1:T(8,128)(2,1)}, u32[]{:S(2)}) copy-start(bf16[1792,576]{0,1:T(8,128)(2,1)} %param.13) | copy-start | bytes 6193156
  7.2 89.1 %all-reduce.2.cloned.1.call-start = ((), (), s32[]{:S(2)}) async-start(), calls=%async_computation | async-start | bytes 655360 | tf_op jit(solution)/shard_map/psum | solution.py:472
  7.2 0.8 copy-start.10
  8.0 1.7 copy-start.12
  9.7 0.7 copy-start.15
  10.4 5.8 %copy-start.24 = (bf16[1,128,1792]{2,1,0:T(8,128)(2,1)S(1)}, bf16[1,128,1792]{2,1,0:T(8,128)(2,1)}, u32[]{:S(2)}) copy-start(bf16[1,128,1792]{2,1,0:T(8,128)(2,1)} %param.12) | copy-start | bytes 1376260
  15.5 2.2 %copy-start.29 = (s32[2]{0:T(128)S(1)}, s32[2]{0:T(128)}, u32[]{:S(2)}) copy-start(s32[2]{0:T(128)} %param.20) | copy-start | bytes 28
  15.5 4.2 %copy-start.30 = (s32[2]{0:T(128)S(1)}, s32[2]{0:T(128)}, u32[]{:S(2)}) copy-start(s32[2]{0:T(128)} %param.21) | copy-start | bytes 28
  15.5 4.8 %copy-start.11 = (s32[2,64,1]{1,2,0:T(1,128)S(1)}, s32[2,64,1]{1,2,0:T(1,128)}, u32[]{:S(2)}) copy-start(s32[2,64,1]{1,2,0:T(1,128)} %param.18) | copy-start | bytes 1540
  15.5 15.5 %collective-permute-start = (bf16[8,32,1152]{2,1,0:T(8,128)(2,1)}, bf16[8,32,1152]{2,1,0:T(8,128)(2,1)}, u32[]{:S(2)}, u32[]{:S(2)}) collective-permute-start(bf16[8,32,1152]{2,1,0:T(8,128)(2,1)} %bitcast.6), channel_id=1, source_target_pairs={{0,2},{2,0},{1,3},{3,1},{4,6},{6,4},{5,7},{7,5},{8,10},{10,8},{9,1... | collective-permute-start | bytes 1769480 | tf_op jit(solution)/shard_map/ppermute | solution.py:453
  31.0 2.3 %collective-permute-start.1 = (bf16[1,8,32,1152]{3,2,1,0:T(8,128)(2,1)}, bf16[1,8,32,1152]{3,2,1,0:T(8,128)(2,1)}, u32[]{:S(2)}, u32[]{:S(2)}) collective-permute-start(bf16[1,8,32,1152]{3,2,1,0:T(8,128)(2,1)} %bitcast.7.mine_ref), channel_id=1, source_target_pairs={{0,1},{1,0},{2,3},{3,2},{4,5},{5,4},{6,7},{7,6},{8,9},{9,8},{10,11... | collective-permute-start | bytes 1769480 | tf_op jit(solution)/shard_map/ppermute | solution.py:457
  39.1 1.4 copy-start.1
  40.6 0.8 copy-start.14
  41.4 15.4 %collective-permute-start.2 = (bf16[8,32,1152]{2,1,0:T(8,128)(2,1)}, bf16[8,32,1152]{2,1,0:T(8,128)(2,1)S(1)}, u32[]{:S(2)}, u32[]{:S(2)}) collective-permute-start(bf16[8,32,1152]{2,1,0:T(8,128)(2,1)} %get-tuple-element.18), channel_id=1, source_target_pairs={{0,4},{5,1},{4,8},{9,5},{8,12},{13,9},{2,6},{7,3},{6,10},{11,7},{1... | collective-permute-start | bytes 1769480 | tf_op jit(solution)/shard_map/ppermute | solution.py:499
  46.2 0.8 copy-start.17
  46.5 33.1 %copy-start.25 = (s32[192]{0:T(256)}, s32[192]{0:T(256)S(1)}, u32[]{:S(2)}) copy-start(s32[192]{0:T(256)S(1)} %select_reduce_fusion) | copy-start | bytes 2308
  46.9 17.8 %collective-permute-start.3 = (bf16[8,32,1152]{2,1,0:T(8,128)(2,1)}, bf16[8,32,1152]{2,1,0:T(8,128)(2,1)S(1)}, u32[]{:S(2)}, u32[]{:S(2)}) collective-permute-start(bf16[8,32,1152]{2,1,0:T(8,128)(2,1)} %copy-done.14), channel_id=1, source_target_pairs={{0,4},{5,1},{4,8},{9,5},{8,12},{13,9},{2,6},{7,3},{6,10},{11,7},{1... | collective-permute-start | bytes 1769480 | tf_op jit(solution)/shard_map/ppermute | solution.py:499
  56.8 1.7 copy-start.2
  60.0 0.8 copy-start.6
  60.8 11.8 %collective-permute-start.4 = (bf16[8,32,1152]{2,1,0:T(8,128)(2,1)S(1)}, bf16[8,32,1152]{2,1,0:T(8,128)(2,1)S(1)}, u32[]{:S(2)}, u32[]{:S(2)}) collective-permute-start(bf16[8,32,1152]{2,1,0:T(8,128)(2,1)S(1)} %queue_chunk.8), channel_id=1, source_target_pairs={{0,4},{5,1},{4,8},{9,5},{8,12},{13,9},{2,6},{7,3},{6,10},{11,7},{1... | collective-permute-start | bytes 1769480 | tf_op jit(solution)/shard_map/ppermute | solution.py:499
  63.7 1.1 copy-start.7
  67.1 10.9 %copy-start.18 = (bf16[1,128,1536]{1,2,0:T(8,128)(2,1)S(1)}, bf16[1,128,1536]{1,2,0:T(8,128)(2,1)}, u32[]{:S(2)}) copy-start(bf16[1,128,1536]{1,2,0:T(8,128)(2,1)} %copy-done.17) | copy-start | bytes 1179652
  67.2 10.9 %copy-start.20 = (bf16[8,128,512]{2,1,0:T(8,128)(2,1)S(1)}, bf16[8,128,512]{2,1,0:T(8,128)(2,1)}, u32[]{:S(2)}) copy-start(bf16[8,128,512]{2,1,0:T(8,128)(2,1)} %param.15) | copy-start | bytes 3145732
  67.2 14.9 %collective-permute-start.8 = (bf16[8,32,1152]{2,1,0:T(8,128)(2,1)}, bf16[8,32,1152]{2,1,0:T(8,128)(2,1)}, u32[]{:S(2)}, u32[]{:S(2)}) collective-permute-start(bf16[8,32,1152]{2,1,0:T(8,128)(2,1)} %queue_chunk.9), channel_id=1, source_target_pairs={{0,4},{5,1},{4,8},{9,5},{8,12},{13,9},{2,6},{7,3},{6,10},{11,7},{1... | collective-permute-start | bytes 1769480 | tf_op jit(solution)/shard_map/ppermute | solution.py:499
  75.1 15.2 %collective-permute-start.9 = (bf16[8,32,1152]{2,1,0:T(8,128)(2,1)}, bf16[8,32,1152]{2,1,0:T(8,128)(2,1)}, u32[]{:S(2)}, u32[]{:S(2)}) collective-permute-start(bf16[8,32,1152]{2,1,0:T(8,128)(2,1)} %queue_chunk.10), channel_id=1, source_target_pairs={{0,4},{5,1},{4,8},{9,5},{8,12},{13,9},{2,6},{7,3},{6,10},{11,7},{1... | collective-permute-start | bytes 1769480 | tf_op jit(solution)/shard_map/ppermute | solution.py:499
  82.1 1.7 copy-start.3
  86.6 8.3 %slice-start = ((s32[192]{0:T(256)}), s32[56]{0:T(128)S(1)}, s32[]{:S(2)}) async-start(s32[192]{0:T(256)} %copy-done.25), calls=%async_computation.1 | async-start | bytes 1024 | tf_op jit(solution)/shard_map/slice | solution.py:518
  86.6 8.4 %copy-start.16 = (bf16[8,128,512]{2,1,0:T(8,128)(2,1)S(1)}, bf16[8,128,512]{2,1,0:T(8,128)(2,1)}, u32[]{:S(2)}) copy-start(bf16[8,128,512]{2,1,0:T(8,128)(2,1)} %convolution_convert_fusion) | copy-start | bytes 3145732
  86.6 8.4 %copy-start.21 = (bf16[8,128,32]{2,1,0:T(8,128)(2,1)S(1)}, bf16[8,128,32]{2,1,0:T(8,128)(2,1)}, u32[]{:S(2)}) copy-start(bf16[8,128,32]{2,1,0:T(8,128)(2,1)} %get-tuple-element.36) | copy-start | bytes 196612
  86.6 12.7 %collective-permute-start.10 = (bf16[8,32,1152]{2,1,0:T(8,128)(2,1)}, bf16[8,32,1152]{2,1,0:T(8,128)(2,1)}, u32[]{:S(2)}, u32[]{:S(2)}) collective-permute-start(bf16[8,32,1152]{2,1,0:T(8,128)(2,1)} %queue_chunk.11), channel_id=1, source_target_pairs={{0,4},{5,1},{4,8},{9,5},{8,12},{13,9},{2,6},{7,3},{6,10},{11,7},{1... | collective-permute-start | bytes 1769480 | tf_op jit(solution)/shard_map/ppermute | solution.py:499
  93.0 12.2 %collective-permute-start.11 = (bf16[8,32,1152]{2,1,0:T(8,128)(2,1)}, bf16[8,32,1152]{2,1,0:T(8,128)(2,1)}, u32[]{:S(2)}, u32[]{:S(2)}) collective-permute-start(bf16[8,32,1152]{2,1,0:T(8,128)(2,1)} %queue_chunk.12), channel_id=1, source_target_pairs={{0,4},{5,1},{4,8},{9,5},{8,12},{13,9},{2,6},{7,3},{6,10},{11,7},{1... | collective-permute-start | bytes 1769480 | tf_op jit(solution)/shard_map/ppermute | solution.py:499
  96.3 12.4 %copy-start.19 = (f32[128,576]{1,0:T(8,128)S(1)}, f32[128,576]{1,0:T(8,128)}, u32[]{:S(2)}) copy-start(f32[128,576]{1,0:T(8,128)} %all-reduce.2.cloned.1.call-done) | copy-start | bytes 884740
  97.4 11.3 %copy-start.26 = (f32[512]{0:T(512)S(1)}, f32[512]{0:T(512)}, u32[]{:S(2)}) copy-start(f32[512]{0:T(512)} %param.14) | copy-start | bytes 6148
  98.7 20.4 %collective-permute-start.5 = (bf16[8,32,1152]{2,1,0:T(8,128)(2,1)}, bf16[8,32,1152]{2,1,0:T(8,128)(2,1)}, u32[]{:S(2)}, u32[]{:S(2)}) collective-permute-start(bf16[8,32,1152]{2,1,0:T(8,128)(2,1)} %copy-done.6), channel_id=1, source_target_pairs={{0,1},{1,0},{2,3},{3,2},{4,5},{5,4},{6,7},{7,6},{8,9},{9,8},{10,11... | collective-permute-start | bytes 1769480 | tf_op jit(solution)/shard_map/ppermute | solution.py:500
  98.8 20.9 %collective-permute-start.6 = (bf16[8,32,1152]{2,1,0:T(8,128)(2,1)S(1)}, bf16[8,32,1152]{2,1,0:T(8,128)(2,1)}, u32[]{:S(2)}, u32[]{:S(2)}) collective-permute-start(bf16[8,32,1152]{2,1,0:T(8,128)(2,1)S(1)} %collective-permute-done.3.refs_4_.refs_1_.refs_0_), channel_id=1, source_target_pairs={{0,1},{1,0},{2,3},{3,2},{4,5},{5,4},{6,7},{7,6},{8,9},{9,8},{10,11... | collective-permute-start | bytes 1769480 | tf_op jit(solution)/shard_map/ppermute | solution.py:500
  99.3 24.0 %collective-permute-start.7 = (bf16[8,32,1152]{2,1,0:T(8,128)(2,1)S(1)}, bf16[8,32,1152]{2,1,0:T(8,128)(2,1)}, u32[]{:S(2)}, u32[]{:S(2)}) collective-permute-start(bf16[8,32,1152]{2,1,0:T(8,128)(2,1)S(1)} %collective-permute-done.4.refs_5_.refs_2_.refs_1_.refs_0_), channel_id=1, source_target_pairs={{0,1},{1,0},{2,3},{3,2},{4,5},{5,4},{6,7},{7,6},{8,9},{9,8},{10,11... | collective-permute-start | bytes 1769480 | tf_op jit(solution)/shard_map/ppermute | solution.py:500
  99.3 26.0 %collective-permute-start.12 = (bf16[8,32,1152]{2,1,0:T(8,128)(2,1)}, bf16[8,32,1152]{2,1,0:T(8,128)(2,1)}, u32[]{:S(2)}, u32[]{:S(2)}) collective-permute-start(bf16[8,32,1152]{2,1,0:T(8,128)(2,1)} %collective-permute-done.8.refs_2_.refs_1_.refs_5_.refs_0_), channel_id=1, source_target_pairs={{0,1},{1,0},{2,3},{3,2},{4,5},{5,4},{6,7},{7,6},{8,9},{9,8},{10,11... | collective-permute-start | bytes 1769480 | tf_op jit(solution)/shard_map/ppermute | solution.py:500
  99.8 1.7 copy-start.4
  105.2 12.1 %collective-permute-start.17 = (bf16[8,32,1152]{2,1,0:T(8,128)(2,1)}, bf16[8,32,1152]{2,1,0:T(8,128)(2,1)}, u32[]{:S(2)}, u32[]{:S(2)}) collective-permute-start(bf16[8,32,1152]{2,1,0:T(8,128)(2,1)} %queue_chunk.13), channel_id=1, source_target_pairs={{0,4},{5,1},{4,8},{9,5},{8,12},{13,9},{2,6},{7,3},{6,10},{11,7},{1... | collective-permute-start | bytes 1769480 | tf_op jit(solution)/shard_map/ppermute | solution.py:499
  111.4 1.7 copy-start.5
  114.9 10.6 %copy-start.22 = (pred[1,2,36864]{2,1,0:T(4,128)(4,1)S(1)}, pred[1,2,36864]{2,1,0:T(4,128)(4,1)}, u32[]{:S(2)}) copy-start(pred[1,2,36864]{2,1,0:T(4,128)(4,1)} %broadcast_in_dim.99) | copy-start | bytes 221188
  114.9 10.6 %copy-start.23 = (bf16[1,2,36864]{2,1,0:T(2,128)(2,1)S(1)}, bf16[1,2,36864]{2,1,0:T(2,128)(2,1)}, u32[]{:S(2)}) copy-start(bf16[1,2,36864]{2,1,0:T(2,128)(2,1)} %convert_element_type.48) | copy-start | bytes 442372
  114.9 22.9 %copy-start.8 = (bf16[8,32,1152]{2,1,0:T(8,128)(2,1)S(1)}, bf16[8,32,1152]{2,1,0:T(8,128)(2,1)}, u32[]{:S(2)}) copy-start(bf16[8,32,1152]{2,1,0:T(8,128)(2,1)} %copy-done.6) | copy-start | bytes 1769476
  114.9 22.9 %copy-start.9 = (bf16[8,128,576]{2,1,0:T(8,128)(2,1)S(1)}, bf16[8,128,576]{2,1,0:T(8,128)(2,1)}, u32[]{:S(2)}) copy-start(bf16[8,128,576]{2,1,0:T(8,128)(2,1)} %pad_maximum_fusion) | copy-start | bytes 3538948
  117.3 9.1 %collective-permute-start.13 = (bf16[8,32,1152]{2,1,0:T(8,128)(2,1)}, bf16[8,32,1152]{2,1,0:T(8,128)(2,1)S(1)}, u32[]{:S(2)}, u32[]{:S(2)}) collective-permute-start(bf16[8,32,1152]{2,1,0:T(8,128)(2,1)} %collective-permute-done.9.refs_2_.refs_6_.refs_1_.refs_0_), channel_id=1, source_target_pairs={{0,1},{1,0},{2,3},{3,2},{4,5},{5,4},{6,7},{7,6},{8,9},{9,8},{10,11... | collective-permute-start | bytes 1769480 | tf_op jit(solution)/shard_map/ppermute | solution.py:500
  119.1 45.2 %collective-permute-start.14 = (bf16[8,32,1152]{2,1,0:T(8,128)(2,1)}, bf16[8,32,1152]{2,1,0:T(8,128)(2,1)S(1)}, u32[]{:S(2)}, u32[]{:S(2)}) collective-permute-start(bf16[8,32,1152]{2,1,0:T(8,128)(2,1)} %collective-permute-done.10.refs_7_.refs_2_.refs_1_.refs_0_), channel_id=1, source_target_pairs={{0,1},{1,0},{2,3},{3,2},{4,5},{5,4},{6,7},{7,6},{8,9},{9,8},{10,11... | collective-permute-start | bytes 1769480 | tf_op jit(solution)/shard_map/ppermute | solution.py:500
  119.7 11.8 %collective-permute-start.18 = (bf16[8,32,1152]{2,1,0:T(8,128)(2,1)S(1)}, bf16[8,32,1152]{2,1,0:T(8,128)(2,1)S(1)}, u32[]{:S(2)}, u32[]{:S(2)}) collective-permute-start(bf16[8,32,1152]{2,1,0:T(8,128)(2,1)S(1)} %queue_chunk.14), channel_id=1, source_target_pairs={{0,4},{5,1},{4,8},{9,5},{8,12},{13,9},{2,6},{7,3},{6,10},{11,7},{1... | collective-permute-start | bytes 1769480 | tf_op jit(solution)/shard_map/ppermute | solution.py:499
  123.2 14.5 %collective-permute-start.19 = (bf16[8,32,1152]{2,1,0:T(8,128)(2,1)S(1)}, bf16[8,32,1152]{2,1,0:T(8,128)(2,1)S(1)}, u32[]{:S(2)}, u32[]{:S(2)}) collective-permute-start(bf16[8,32,1152]{2,1,0:T(8,128)(2,1)S(1)} %queue_chunk.15), channel_id=1, source_target_pairs={{0,4},{5,1},{4,8},{9,5},{8,12},{13,9},{2,6},{7,3},{6,10},{11,7},{1... | collective-permute-start | bytes 1769480 | tf_op jit(solution)/shard_map/ppermute | solution.py:499
  125.3 41.4 %collective-permute-start.15 = (bf16[8,32,1152]{2,1,0:T(8,128)(2,1)}, bf16[8,32,1152]{2,1,0:T(8,128)(2,1)S(1)}, u32[]{:S(2)}, u32[]{:S(2)}) collective-permute-start(bf16[8,32,1152]{2,1,0:T(8,128)(2,1)} %collective-permute-done.11.refs_8_.refs_2_.refs_1_), channel_id=1, source_target_pairs={{0,1},{1,0},{2,3},{3,2},{4,5},{5,4},{6,7},{7,6},{8,9},{9,8},{10,11... | collective-permute-start | bytes 1769480 | tf_op jit(solution)/shard_map/ppermute | solution.py:500
  126.3 52.5 %collective-permute-start.20 = (bf16[8,32,1152]{2,1,0:T(8,128)(2,1)}, bf16[8,32,1152]{2,1,0:T(8,128)(2,1)S(1)}, u32[]{:S(2)}, u32[]{:S(2)}) collective-permute-start(bf16[8,32,1152]{2,1,0:T(8,128)(2,1)} %collective-permute-done.17.refs_2_.refs_9_), channel_id=1, source_target_pairs={{0,1},{1,0},{2,3},{3,2},{4,5},{5,4},{6,7},{7,6},{8,9},{9,8},{10,11... | collective-permute-start | bytes 1769480 | tf_op jit(solution)/shard_map/ppermute | solution.py:500
  131.4 47.4 %collective-permute-start.21 = (bf16[8,32,1152]{2,1,0:T(8,128)(2,1)S(1)}, bf16[8,32,1152]{2,1,0:T(8,128)(2,1)S(1)}, u32[]{:S(2)}, u32[]{:S(2)}) collective-permute-start(bf16[8,32,1152]{2,1,0:T(8,128)(2,1)S(1)} %collective-permute-done.18.refs_10_), channel_id=1, source_target_pairs={{0,1},{1,0},{2,3},{3,2},{4,5},{5,4},{6,7},{7,6},{8,9},{9,8},{10,11... | collective-permute-start | bytes 1769480 | tf_op jit(solution)/shard_map/ppermute | solution.py:500
  137.7 41.1 %collective-permute-start.22 = (bf16[8,32,1152]{2,1,0:T(8,128)(2,1)S(1)}, bf16[8,32,1152]{2,1,0:T(8,128)(2,1)S(1)}, u32[]{:S(2)}, u32[]{:S(2)}) collective-permute-start(bf16[8,32,1152]{2,1,0:T(8,128)(2,1)S(1)} %collective-permute-done.19.refs_11_), channel_id=1, source_target_pairs={{0,1},{1,0},{2,3},{3,2},{4,5},{5,4},{6,7},{7,6},{8,9},{9,8},{10,11... | collective-permute-start | bytes 1769480 | tf_op jit(solution)/shard_map/ppermute | solution.py:500
  164.3 2.4 %copy-start.27 = (bf16[8,32,1152]{2,1,0:T(8,128)(2,1)}, bf16[8,32,1152]{2,1,0:T(8,128)(2,1)S(1)}, u32[]{:S(2)}) copy-start(bf16[8,32,1152]{2,1,0:T(8,128)(2,1)S(1)} %collective-permute-done.14.refs_11_) | copy-start | bytes 1769476
  164.3 14.5 %collective-permute-start.16 = (bf16[128,576]{1,0:T(8,128)(2,1)S(1)}, bf16[128,576]{1,0:T(8,128)(2,1)S(1)}, u32[]{:S(2)}, u32[]{:S(2)}) collective-permute-start(bf16[128,576]{1,0:T(8,128)(2,1)S(1)} %get-tuple-element.30.refs_7_), channel_id=1, source_target_pairs={{0,1},{2,3},{4,5},{6,7},{8,9},{10,11},{12,13},{14,15},{16,17},{18,... | collective-permute-start | bytes 442376 | tf_op jit(solution)/shard_map/ppermute | solution.py:18
  166.8 0.8 copy-start.28
  167.6 11.3 %copy-start.13 = (bf16[8,512,128]{2,1,0:T(8,128)(2,1)S(1)}, bf16[8,512,128]{2,1,0:T(8,128)(2,1)}, u32[]{:S(2)}) copy-start(bf16[8,512,128]{2,1,0:T(8,128)(2,1)} %refs_8_.1) | copy-start | bytes 3145732
Sparse Core Ops, SparseCore 0:
  17.8 37.6 all-reduce.1

commit v4 on v0

v4 whole, which is shorter than its diff:
```python
import functools
import math

import jax
import jax.numpy as jnp
from jax import lax
from jax.experimental import pallas as pl
from jax.experimental.pallas import tpu as pltpu
from jax.sharding import PartitionSpec as P

LOWEST = -1e30
VMEM_LIMIT = 48 * 1024 * 1024


def from_behind(block, axis, distance):
    devices = range(lax.axis_size(axis))
    route = [(i - distance, i) for i in devices if i - distance in devices]
    return lax.ppermute(block, axis, route)


def rotate(vector, cosine_table, sine_table):
    half_width = vector.shape[-1] // 2
    first_half = vector[..., :half_width]
    second_half = vector[..., half_width:]
    return jnp.concatenate(
        [
            first_half * cosine_table - second_half * sine_table,
            first_half * sine_table + second_half * cosine_table,
        ],
        axis=-1,
    )


def angles(positions, rope_width):
    half_width = rope_width // 2
    frequency = 10000.0 ** (-2.0 * jnp.arange(half_width, dtype=jnp.float32) / rope_width)
    phases = positions.astype(jnp.float32)[:, None] * frequency[None, :]
    return (jnp.cos(phases), jnp.sin(phases))


def finish_latent(summed, positions, live_rows, kv_gain, latent_width):
    latent_part = summed[:, :latent_width]
    mean_square = jnp.mean(latent_part * latent_part, axis=-1, keepdims=True)
    normed = latent_part * lax.rsqrt(mean_square + 1e-06) * kv_gain
    cosine_table, sine_table = angles(positions, summed.shape[1] - latent_width)
    rotated = rotate(summed[:, latent_width:], cosine_table, sine_table)
    joined = jnp.concatenate([normed, rotated], axis=-1).astype(jnp.bfloat16)
    return jnp.where(live_rows[:, None], joined, jnp.zeros_like(joined))


def any_spec():
    return pl.BlockSpec(memory_space=pl.ANY)


def smem_spec():
    return pl.BlockSpec(memory_space=pltpu.SMEM)


def vmem_spec():
    return pl.BlockSpec(memory_space=pltpu.VMEM)


def pick_kernel(
    cap, owner_hbm, slot_hbm, pool_hbm, count_ref, first_ref, rest_ref, foreign_ref,
    owner_ref, slot_ref, pool_ref, pages, lists, sems,
):
    n_req = lax.axis_size("req")
    head_idx = lax.axis_index("head")
    req_idx = lax.axis_index("req")
    seq_idx = lax.axis_index("seq")
    n_pages = owner_ref.shape[1]
    pool_pages, pairs, pair_width = pages.shape
    chunk = first_ref.shape[0]
    width = pool_ref.shape[1]
    loads = [
        pltpu.make_async_copy(owner_hbm, owner_ref, sems.at[0]),
        pltpu.make_async_copy(slot_hbm, slot_ref, sems.at[1]),
        pltpu.make_async_copy(
            pool_hbm.at[:, pl.ds(pl.multiple_of(seq_idx * width, 128), width)], pool_ref, sems.at[2]
        ),
    ]
    for load in loads:
        load.start()
    loads[0].wait()
    loads[1].wait()
    self_owner = head_idx * n_req + req_idx
    founds = []
    for shift in range(n_req):
        request = lax.rem(req_idx + shift, n_req)

        def note(page, found, shift=shift, request=request):
            lists[shift, found] = slot_ref[request, page]
            return found + (owner_ref[request, page] == self_owner).astype(jnp.int32)

        founds.append(lax.fori_loop(0, n_pages, note, jnp.int32(0), unroll=8))

    def tally(page, counts):
        owner = owner_ref[req_idx, page]
        return tuple(
            counts[shift]
            + (owner == head_idx * n_req + lax.rem(req_idx + n_req - shift, n_req)).astype(jnp.int32)
            for shift in range(n_req)
        )

    counts = lax.fori_loop(0, n_pages, tally, (jnp.int32(0),) * n_req, unroll=8)
    for shift in range(n_req):
        count_ref[shift] = counts[shift]
    loads[2].wait()
    step = 16
    row = lax.broadcasted_iota(jnp.int32, (step * step, step * step), 0)
    column = lax.broadcasted_iota(jnp.int32, (step * step, step * step), 1)
    swap = ((row // step == column % step) & (row % step == column // step)).astype(jnp.bfloat16)
    for page in range(0, pool_pages, step):
        for pair in range(0, pairs, step):
            rows = jnp.concatenate(
                [
                    pool_ref[page : page + step, (pair + i) * pair_width : (pair + i + 1) * pair_width]
                    for i in range(step)
                ],
                axis=0,
            )
            turned = jnp.dot(swap, rows, preferred_element_type=jnp.float32).astype(jnp.bfloat16)
            pages[page : page + step, pair : pair + step, :] = turned.reshape(step, step, pair_width)
    for shift in range(n_req):
        for rank in range(cap):
            slot = jnp.where(rank < founds[shift], lists[shift, rank], 0)
            if shift > 0:
                target, sem = foreign_ref.at[shift - 1, rank], sems.at[3]
            elif rank < chunk:
                target, sem = first_ref.at[rank], sems.at[4]
            else:
                target, sem = rest_ref.at[rank - chunk], sems.at[5]
            pltpu.make_async_copy(pages.at[slot], target, sem).start()
    pltpu.make_async_copy(foreign_ref, foreign_ref, sems.at[3]).wait()
    pltpu.make_async_copy(first_ref, first_ref, sems.at[4]).wait()
    if cap > chunk:
        pltpu.make_async_copy(rest_ref, rest_ref, sems.at[5]).wait()


def pick_pages(page_owner, page_slot, page_pool, cap, chunk, n_req, n_seq, pairs):
    pool_pages, page_width = page_pool.shape
    page = (pairs // n_seq, page_width // pairs)
    return pl.pallas_call(
        functools.partial(pick_kernel, cap),
        out_shape=(
            jax.ShapeDtypeStruct((n_req,), jnp.int32),
            jax.ShapeDtypeStruct((chunk, *page), jnp.bfloat16),
            jax.ShapeDtypeStruct((max(1, cap - chunk), *page), jnp.bfloat16),
            jax.ShapeDtypeStruct((n_req - 1, cap, *page), jnp.bfloat16),
        ),
        in_specs=[any_spec(), any_spec(), any_spec()],
        out_specs=(smem_spec(), any_spec(), any_spec(), any_spec()),
        scratch_shapes=[
            pltpu.SMEM(page_owner.shape, jnp.int32),
            pltpu.SMEM(page_slot.shape, jnp.int32),
            pltpu.VMEM((pool_pages, page_width // n_seq), jnp.bfloat16),
            pltpu.VMEM((pool_pages, *page), jnp.bfloat16),
            pltpu.SMEM((n_req, cap + 1), jnp.int32),
            pltpu.SemaphoreType.DMA((6,)),
        ],
        compiler_params=pltpu.CompilerParams(vmem_limit_bytes=VMEM_LIMIT),
        cost_estimate=pl.CostEstimate(flops=10**9, bytes_accessed=6 * 10**6, transcendentals=0),
        name="pick_pages",
    )(page_owner, page_slot, page_pool)


def join_kernel(chunk, cap, count_ref, rest_ref, *refs):
    n_req = count_ref.shape[0]
    foreign, targets, sems = refs[: n_req - 1], refs[n_req - 1 : -1], refs[-1]
    excess = jnp.maximum(count_ref[0] - chunk, 0)
    for j in range(chunk * len(targets)):
        part, place = divmod(j, chunk)

        def fetch(condition, source):
            @pl.when(condition)
            def _():
                pltpu.make_async_copy(source, targets[part].at[place], sems.at[part]).start()

        rank = jnp.int32(j)
        taken = rank < excess
        if cap > chunk:
            fetch(taken, rest_ref.at[jnp.minimum(rank, cap - chunk - 1)])
        rank = rank - excess
        for shift in range(1, n_req):
            here = jnp.logical_not(taken) & (rank < count_ref[shift])
            fetch(here, foreign[shift - 1].at[jnp.clip(rank, 0, cap - 1)])
            taken = taken | here
            rank = rank - count_ref[shift]
        fetch(jnp.logical_not(taken), foreign[0].at[0])
    for part, target in enumerate(targets):
        pltpu.make_async_copy(target, target, sems.at[part]).wait()


def join_pages(counts, rest, foreign, chunk, cap, parts):
    shape = jax.ShapeDtypeStruct((chunk, *rest.shape[1:]), jnp.bfloat16)
    return pl.pallas_call(
        functools.partial(join_kernel, chunk, cap),
        out_shape=(shape,) * parts,
        in_specs=[smem_spec()] + [any_spec()] * (1 + len(foreign)),
        out_specs=(vmem_spec(),) * parts,
        scratch_shapes=[pltpu.SemaphoreType.DMA((parts,))],
        compiler_params=pltpu.CompilerParams(vmem_limit_bytes=VMEM_LIMIT),
        cost_estimate=pl.CostEstimate(flops=0, bytes_accessed=3 * 10**6, transcendentals=0),
        name="join_pages",
    )(counts, rest, *foreign)


def token_limits(owners, prefix, req_idx, n_head, n_req, chunk, parts, page_len):
    pages = owners.shape[0]
    order = jnp.arange(pages, dtype=jnp.int32)
    place = owners // n_req
    shift = lax.rem(req_idx + n_req - lax.rem(owners, n_req), n_req)
    key = shift * pages + order
    together = place[None, :] == place[:, None]
    rank = jnp.sum((together & (key[None, :] < key[:, None])).astype(jnp.int32), axis=1)
    held = jnp.sum((together & (shift[None, :] == 0)).astype(jnp.int32), axis=1)
    later = rank - jnp.minimum(held, chunk)
    early = (shift == 0) & (rank < chunk)
    part = jnp.where(early, 0, 1 + later // chunk)
    within = jnp.where(early, rank, lax.rem(later, chunk))
    slot = (part * n_head + place) * chunk + within
    tokens = jnp.clip(prefix - order * page_len, 0, page_len)
    slots = jnp.arange(parts * n_head * chunk, dtype=jnp.int32)
    limits = jnp.sum(jnp.where(slot[None, :] == slots[:, None], tokens[None, :], 0), axis=1)
    return limits


def score_rows(q_ref, key_block, target, mark_of, highest, weight_sum, rows, tile, scale, mask_of):
    for start in range(0, rows, tile):
        part = slice(start, start + tile)
        scores = lax.dot_general(
            q_ref[part, :], key_block[...], (((1,), (1,)), ((), ())), preferred_element_type=jnp.float32
        )
        scores = mask_of(scores * scale, start)
        old = highest[part, :]
        new = jnp.maximum(old, jnp.max(scores, axis=1, keepdims=True))
        weights = jnp.exp2(scores - new)
        highest[part, :] = new
        weight_sum[part, :] = weight_sum[part, :] * jnp.exp2(old - new) + jnp.sum(
            weights, axis=1, keepdims=True
        )
        target[part, :] = weights
        mark_of(part, new)


def block_bias(limit_ref, block, chunk, n_seq, half_pairs, block_keys):
    pair_rows = block_keys // 2
    lane = lax.broadcasted_iota(jnp.int32, (1, block_keys), 1)
    row = lax.rem(lane, pair_rows)
    slot = lax.rem(row // half_pairs, chunk)
    token = 2 * (lax.rem(row, half_pairs) + (row // (chunk * half_pairs)) * half_pairs) + lane // pair_rows
    limit = jnp.zeros_like(lane)
    for j in range(chunk):
        limit = jnp.where(slot == j, limit_ref[block * chunk + j], limit)
    return jnp.where(token < limit, 0.0, -jnp.inf)


def any_token(limit_ref, block, chunk):
    return functools.reduce(jnp.maximum, [limit_ref[block * chunk + j] for j in range(chunk)]) > 0


def load_block(block_ref, keys, key_width):
    pair_rows = keys.shape[0] // 2
    page_rows = block_ref[...].reshape(pair_rows, block_ref.shape[-1])
    keys[:pair_rows, :] = page_rows[:, :key_width]
    keys[pair_rows:, :] = page_rows[:, key_width:]


def set_mark(marks, part, block, value):
    column = lax.broadcasted_iota(jnp.int32, (value.shape[0], marks.shape[1]), 1)
    marks[part, :] = jnp.where(column == block, value, marks[part, :])


def score_kernel(shape, number, limit_ref, q_ref, *refs):
    rows, tile, scale, chunk, n_seq, n_head = shape
    refs = list(refs)
    if number > 0:
        marks_in, sum_in, high_in = [refs.pop(0) for _ in range(3)]
        refs.pop(0), refs.pop(0)
    gathered = refs.pop(0)
    weights_ref, values_ref, marks, weight_sum, highest = [refs.pop(0) for _ in range(5)]
    blocks, keys, weights, load_sems, value_sems, weight_sems = refs
    block_keys, key_width = keys.shape[1:]
    latent_width = values_ref.shape[2]
    half_pairs = blocks.shape[3]

    def load(head):
        return pltpu.make_async_copy(gathered.at[head], blocks.at[head], load_sems.at[head])

    def value_store(head):
        return pltpu.make_async_copy(
            keys.at[head, :, pl.ds(0, latent_width)], values_ref.at[number * n_head + head], value_sems.at[head]
        )

    def weight_store(head):
        return pltpu.make_async_copy(
            weights.at[head], weights_ref.at[number * n_head + head], weight_sems.at[head]
        )

    for head in range(n_head):
        load(head).start()
    if number > 0:
        marks[...] = marks_in[...]
        weight_sum[...] = sum_in[...]
        highest[...] = high_in[...]
    else:
        marks[...] = jnp.zeros_like(marks)
        weight_sum[...] = jnp.zeros_like(weight_sum)
        highest[...] = jnp.full_like(highest, LOWEST)

    def one_block(head, carry):
        load(head).wait()
        load_block(blocks.at[head], keys.at[head], key_width)
        value_store(head).start()

        @pl.when(any_token(limit_ref, head, chunk))
        def _():
            bias = block_bias(limit_ref, head, chunk, n_seq, half_pairs, block_keys)
            score_rows(
                q_ref, keys.at[head], weights.at[head],
                lambda part, new: set_mark(marks, part, number * n_head + head, new),
                highest, weight_sum, rows, tile, scale, lambda scores, start: scores + bias,
            )

        weight_store(head).start()
        return carry

    lax.fori_loop(0, n_head, one_block, 0)
    for head in range(n_head):
        value_store(head).wait()
        weight_store(head).wait()


def score_part(number, parts, limits, q_rows, gathered, state, shape, latent_width):
    rows, tile, scale, chunk, n_seq, n_head = shape
    key_width = q_rows.shape[1]
    _, _, half_pairs, pair_width = gathered.shape[1:]
    block_keys = 2 * n_seq * chunk * half_pairs
    total = (parts - 1) * n_head
    out_shape = (
        jax.ShapeDtypeStruct((total, rows, block_keys), jnp.float32),
        jax.ShapeDtypeStruct((total, block_keys, latent_width), jnp.bfloat16),
        jax.ShapeDtypeStruct((rows, total), jnp.float32),
        jax.ShapeDtypeStruct((rows, 1), jnp.float32),
        jax.ShapeDtypeStruct((rows, 1), jnp.float32),
    )
    operands = [limits, q_rows]
    specs = [smem_spec(), vmem_spec()]
    aliases = {}
    if number > 0:
        operands += [state[2], state[3], state[4], state[0], state[1]]
        specs += [vmem_spec()] * 3 + [any_spec()] * 2
        aliases = {5: 0, 6: 1}
    operands.append(gathered)
    specs.append(any_spec())
    work = n_head * block_keys * rows
    return pl.pallas_call(
        functools.partial(score_kernel, shape, number),
        out_shape=out_shape,
        in_specs=specs,
        out_specs=(any_spec(), any_spec(), vmem_spec(), vmem_spec(), vmem_spec()),
        scratch_shapes=[
            pltpu.VMEM((n_head, n_seq, chunk, half_pairs, pair_width), jnp.bfloat16),
            pltpu.VMEM((n_head, block_keys, key_width), jnp.bfloat16),
            pltpu.VMEM((n_head, rows, block_keys), jnp.float32),
            pltpu.SemaphoreType.DMA((n_head,)),
            pltpu.SemaphoreType.DMA((n_head,)),
            pltpu.SemaphoreType.DMA((n_head,)),
        ],
        input_output_aliases=aliases,
        compiler_params=pltpu.CompilerParams(vmem_limit_bytes=VMEM_LIMIT),
        cost_estimate=pl.CostEstimate(
            flops=2 * work * key_width, bytes_accessed=10**7, transcendentals=work
        ),
        name="score_part",
    )(*operands)


def finish_kernel(
    shape, depth, limit_ref, q_ref, marks, sum_in, high_in, weights_hbm, values_hbm, gathered,
    suffix_ref, earlier_ref, fresh_ref, up_ref, out_ref,
    weight_sum, highest, total, blocks, keys, last_weights, last_marks, near_keys, near_weights, near_mark,
    weights, values, load_sems, weight_sems, value_sems,
):
    rows, tile, scale, chunk, n_seq, n_head = shape
    n_blocks = weights_hbm.shape[0]
    block_keys, key_width = keys.shape[1:]
    latent_width = total.shape[1]
    half_pairs = blocks.shape[3]
    half_len = earlier_ref.shape[0]
    seq_idx = lax.axis_index("seq")
    live = suffix_ref[0]

    def load(head):
        return pltpu.make_async_copy(gathered.at[head], blocks.at[head], load_sems.at[head])

    def fetches(block):
        place = lax.rem(block, depth)
        return (
            pltpu.make_async_copy(weights_hbm.at[block], weights.at[place], weight_sems.at[place]),
            pltpu.make_async_copy(values_hbm.at[block], values.at[place], value_sems.at[place]),
        )

    def fetch(block):
        for copy in fetches(block):
            copy.start()

    for head in range(n_head):
        load(head).start()
    for block in range(min(depth, n_blocks)):
        fetch(block)
    weight_sum[...] = sum_in[...]
    highest[...] = high_in[...]
    near_keys[:half_len, :] = earlier_ref[...]
    near_keys[half_len:, :] = fresh_ref[...]

    def near(scores, start):
        row = lax.broadcasted_iota(jnp.int32, scores.shape, 0) + start
        place = lax.broadcasted_iota(jnp.int32, scores.shape, 1) + (seq_idx - 1) * half_len
        query = lax.rem(row, half_len) + seq_idx * half_len
        allowed = (place >= 0) & (place <= query) & (place < live)
        return jnp.where(allowed, scores, -jnp.inf)

    def near_note(part, new):
        near_mark[part, :] = new

    score_rows(
        q_ref, near_keys, near_weights, near_note, highest, weight_sum, rows, tile, scale, near
    )
    last_base = n_blocks

    def one_score(head, carry):
        load(head).wait()

        @pl.when(any_token(limit_ref, last_base + head, chunk))
        def _():
            load_block(blocks.at[head], keys.at[head], key_width)
            bias = block_bias(limit_ref, last_base + head, chunk, n_seq, half_pairs, block_keys)
            score_rows(
                q_ref, keys.at[head], last_weights.at[head],
                lambda part, new: set_mark(last_marks, part, head, new),
                highest, weight_sum, rows, tile, scale, lambda scores, start: scores + bias,
            )

        return carry

    last_marks[...] = jnp.zeros_like(last_marks)
    lax.fori_loop(0, n_head, one_score, 0)

    def add_block(weight_block, value_block, mark_of):
        for start in range(0, rows, tile):
            part = slice(start, start + tile)
            factor = jnp.exp2(mark_of(part) - highest[part, :]) / weight_sum[part, :]
            total[part, :] += jnp.dot(
                (weight_block[part, :] * factor).astype(jnp.bfloat16),
                value_block,
                preferred_element_type=jnp.float32,
            )

    def mark_column(table, block):
        def mark_of(part):
            chosen = table[part, :]
            column = lax.broadcasted_iota(jnp.int32, chosen.shape, 1)
            return jnp.sum(jnp.where(column == block, chosen, 0.0), axis=1, keepdims=True)

        return mark_of

    total[...] = jnp.zeros_like(total)
    add_block(near_weights, near_keys[:, :latent_width], lambda part: near_mark[part, :])

    def one_add(block, carry):
        for copy in fetches(block):
            copy.wait()

        @pl.when(any_token(limit_ref, block, chunk))
        def _():
            place = lax.rem(block, depth)
            add_block(weights.at[place], values[place], mark_column(marks, block))

        @pl.when(block + depth < n_blocks)
        def _():
            fetch(block + depth)

        return carry

    lax.fori_loop(0, n_blocks, one_add, 0)

    def one_last(head, carry):
        @pl.when(any_token(limit_ref, last_base + head, chunk))
        def _():
            add_block(
                last_weights.at[head], keys[head, :, :latent_width], mark_column(last_marks, head)
            )

        return carry

    lax.fori_loop(0, n_head, one_last, 0)
    heads, _, value_width = up_ref.shape
    steps = lax.broadcasted_iota(jnp.int32, (half_len, value_width), 0) + seq_idx * half_len
    for head in range(heads):
        latent = total[head * half_len : (head + 1) * half_len, :].astype(jnp.bfloat16)
        raised = jnp.dot(latent, up_ref[head], preferred_element_type=jnp.float32)
        out_ref[:, head * value_width : (head + 1) * value_width] = jnp.where(
            steps < live, raised, 0.0
        ).astype(jnp.bfloat16)


def finish(limits, q_rows, state, gathered, suffix, earlier, fresh, up_weight, shape):
    rows, tile, scale, chunk, n_seq, n_head = shape
    weights, values, marks, weight_sum, highest = state
    key_width = q_rows.shape[1]
    n_blocks, block_keys, latent_width = values.shape
    half_len = fresh.shape[0]
    heads, _, value_width = up_weight.shape
    depth = min(4, n_blocks)
    column = pltpu.VMEM((rows, 1), jnp.float32)
    work = (n_blocks + n_head) * block_keys * rows
    return pl.pallas_call(
        functools.partial(finish_kernel, shape, depth),
        out_shape=jax.ShapeDtypeStruct((half_len, heads * value_width), jnp.bfloat16),
        in_specs=[smem_spec()] + [vmem_spec()] * 4 + [any_spec()] * 3 + [smem_spec()] + [vmem_spec()] * 3,
        out_specs=vmem_spec(),
        scratch_shapes=[
            column,
            column,
            pltpu.VMEM((rows, latent_width), jnp.float32),
            pltpu.VMEM(gathered.shape, jnp.bfloat16),
            pltpu.VMEM((n_head, block_keys, key_width), jnp.bfloat16),
            pltpu.VMEM((n_head, rows, block_keys), jnp.float32),
            pltpu.VMEM((rows, n_head), jnp.float32),
            pltpu.VMEM((2 * half_len, key_width), jnp.bfloat16),
            pltpu.VMEM((rows, 2 * half_len), jnp.float32),
            column,
            pltpu.VMEM((depth, rows, block_keys), jnp.float32),
            pltpu.VMEM((depth, block_keys, latent_width), jnp.bfloat16),
            pltpu.SemaphoreType.DMA((n_head,)),
            pltpu.SemaphoreType.DMA((depth,)),
            pltpu.SemaphoreType.DMA((depth,)),
        ],
        compiler_params=pltpu.CompilerParams(vmem_limit_bytes=VMEM_LIMIT),
        cost_estimate=pl.CostEstimate(
            flops=2 * work * latent_width, bytes_accessed=3 * 10**7, transcendentals=work // 4
        ),
        name="finish",
    )(
        limits, q_rows, marks, weight_sum, highest, weights, values, gathered,
        suffix, earlier, fresh, up_weight,
    )


def local(
    queries,
    hidden,
    w_dkv,
    kv_gain,
    w_uk,
    value_up_weight,
    page_pool,
    page_owner,
    page_slot,
    prefix_len,
    suffix_len,
):
    n_head = lax.axis_size("head")
    n_req = lax.axis_size("req")
    n_seq = lax.axis_size("seq")
    req_idx = lax.axis_index("req")
    seq_idx = lax.axis_index("seq")
    _, half_len, d_local = hidden.shape
    heads_dev, nope_width, latent_width = w_uk.shape
    lat_width = w_dkv.shape[1]
    rope_width = lat_width - latent_width
    query_width = queries.shape[2] // heads_dev
    page_width = page_pool.shape[1]
    page_len = page_width // lat_width
    pairs = page_len // 2
    pages_req = page_slot.shape[1]
    cap = max(2, 2 * pages_req // (n_head * n_req))
    parts = 4
    chunk = n_req * cap // parts
    score_scale = float(query_width) ** (-0.5)

    owner_rows = page_owner[:, :, 0]
    counts, first, rest, foreign = pick_pages(
        owner_rows, page_slot, page_pool, cap, chunk, n_req, n_seq, pairs
    )
    gather = functools.partial(lax.all_gather, axis_name=("head", "seq"), axis=0, tiled=False)
    gathered = [gather(first)]
    arrived = [
        lax.ppermute(foreign[s - 1], "req", [(i, (i + s) % n_req) for i in range(n_req)])
        for s in range(1, n_req)
    ]
    joined = join_pages(counts, rest, arrived, chunk, cap, parts - 1)
    gathered += [gather(part) for part in joined]
    gathered = [g.reshape(n_head, n_seq, *g.shape[1:]) for g in gathered]

    my_prefix = lax.dynamic_index_in_dim(prefix_len, req_idx, 0, keepdims=False)
    my_suffix = lax.dynamic_index_in_dim(suffix_len, req_idx, 0, keepdims=False)
    own_owners = lax.dynamic_index_in_dim(owner_rows, req_idx, 0, keepdims=False)
    limits = token_limits(own_owners, my_prefix, req_idx, n_head, n_req, chunk, parts, page_len)
    local_t = jnp.arange(half_len, dtype=jnp.int32)
    glob_t = seq_idx * half_len + local_t
    positions = my_prefix + glob_t
    live_rows = glob_t < my_suffix

    partial_value = jnp.dot(hidden[0], w_dkv, preferred_element_type=jnp.float32)
    summed = lax.psum(partial_value, "head")
    fresh = finish_latent(summed, positions, live_rows, kv_gain, latent_width)
    new_pages = fresh.reshape(1, half_len // page_len, page_len * lat_width)
    earlier = from_behind(fresh, "seq", 1)

    query_rows = queries[0].reshape(half_len, heads_dev, query_width)
    q_latent = jnp.einsum(
        "thn,hnk->htk", query_rows[..., :nope_width], w_uk, preferred_element_type=jnp.float32
    ).astype(jnp.bfloat16)
    cosine_table, sine_table = angles(positions, rope_width)
    q_rotated = rotate(
        jnp.swapaxes(query_rows[..., nope_width:], 0, 1).astype(jnp.float32), cosine_table, sine_table
    ).astype(jnp.bfloat16)
    rows = heads_dev * half_len
    q_rows = jnp.concatenate([q_latent, q_rotated], axis=-1).reshape(rows, lat_width)

    tile = 256 if rows % 256 == 0 else rows
    shape = (rows, tile, score_scale * math.log2(math.e), chunk, n_seq, n_head)
    state = None
    part_slots = n_head * chunk
    for number in range(parts - 1):
        part_limits = limits[number * part_slots : (number + 1) * part_slots]
        state = score_part(
            number, parts, part_limits, q_rows, gathered[number], state, shape, latent_width
        )
    attn_out = finish(
        limits, q_rows, state, gathered[-1], my_suffix.reshape(1), earlier, fresh, value_up_weight, shape
    )
    return (attn_out[None], new_pages)


def solution(mesh):
    placed = (
        P(("groups", "req"), "seq", "head"),
        P(("groups", "req"), "seq", "head"),
        P("head", None),
        P(),
        P("head", None, None),
        P("head", None, None),
        P(("groups", "head", "req"), None),
        P("groups", None, None),
        P("groups", None),
        P("groups"),
        P("groups"),
    )
    return jax.shard_map(
        local,
        mesh=mesh,
        in_specs=placed,
        out_specs=(P(("groups", "req"), "seq", "head"), P(("groups", "req"), "seq", None)),
        check_vma=False,
    )
```

time: 324 us -> 186 us (0.57)
  waiting for transfers between devices: 187 us -> 66.6 us
  Pallas kernels: 0 us -> 54.7 us
  other arithmetic: 48 us -> 11 us
  matrix products: 27.4 us -> 3.06 us
  local copies, waits for them, and re-layouts: 40.5 us -> 28 us
    all_gather x1 -> x4, waiting for transfers between devices: 161 us -> 39.5 us  [the longest x3 39.5 us: local(): gathered += [gather(part) for part in joined]]
    pallas_call x0 -> x6, Pallas kernels: none -> 54.7 us  [the longest x3 24.7 us: score_part(): pl.pallas_call(functools.partial(score_kernel, shape, number), out_shape=...]
    all_to_all x1 -> x0, waiting for transfers between devices: 25.5 us -> none  [local(): lax.all_to_all(outgoing, 'req', split_axis=0, concat_axis=0, tiled=True)]
    dot_general x4 -> x2, matrix products: 27.4 us -> 3.06 us  [the longest x1 2.57 us: local(): jnp.dot(hidden[0], w_dkv, preferred_element_type=jnp.float32)]
    sub x1 -> x0, other arithmetic: 22.9 us -> none  [local(): exponent = jnp.exp(scores - row_max)]
    unnamed x19 -> x62, local copies, waits for them, and re-layouts: 2.65 us -> 23.9 us
    gather x2 -> x0, local copies, waits for them, and re-layouts: 18.2 us -> none  [the longest x1 14.7 us: local(): received.reshape(owners * slot_cap, page_width)]
    another operation x2 -> x0, local copies, waits for them, and re-layouts: 17.5 us -> none  [local(): cached[0]]
  transfers between devices with their start and end apart: 4 -> 7, of which waited for: 3 -> 5; matrix products, arithmetic and copies ran while one was open for 16% -> 9% of each run, Pallas kernels for 0% -> 17%
where the time goes in v4:
time: 186 us; the launch traced here: 184 us
  waiting for transfers between devices  66.6 us (36%)
  Pallas kernels  54.7 us (29%)
  local copies, waits for them, and re-layouts  28 us (15%)
  between operations  16 us (9%)
  other arithmetic  11 us (6%)
  starting transfers between devices  5.16 us (3%)
  matrix products  3.06 us (2%)
    all_gather x3, waiting for transfers between devices, local(): gathered += [gather(part) for part in joined]  39.5 us
    pallas_call x3, Pallas kernels, score_part(): pl.pallas_call(functools.partial(score_kernel, shape, number), out_shape=...  24.7 us
    unnamed x62, local copies, waits for them, and re-layouts  23.9 us
    pallas_call x1, Pallas kernels, finish(): pl.pallas_call(functools.partial(finish_kernel, shape, depth), out_shape=...  22.8 us
    ppermute x1, waiting for transfers between devices, local(): lax.ppermute(foreign[s - 1], 'req', [(i, (i + s) % n_req) for i in range(...  13.3 us
    psum x1, waiting for transfers between devices, local(): summed = lax.psum(partial_value, 'head')  13.2 us
    pallas_call x1, Pallas kernels, pick_pages(): pl.pallas_call(functools.partial(pick_kernel, cap), out_shape=(jax.ShapeD...  4.14 us
  transfers between devices with their start and end apart: 7, of which 5 were waited for; matrix products, arithmetic and copies ran while one was open for 9% of the time, Pallas kernels for 17%

profile of v4, /device:TPU:0, one launch (start us, length us, event | category | flops | bytes accessed | tf_op | source)
XLA Modules:
  0.0 184.4 jit_solution(892152892659977637)
XLA Ops:
  8.1 1.5 copy-done
  9.6 2.6 %fusion = f32[128,576]{1,0:T(8,128)} fusion(bf16[1792,576]{0,1:T(8,128)(2,1)S(1)} %copy-done, bf16[1,128,1792]{2,1,0:T(8,128)(2,1)} %param.12), kind=kOutput, calls=%fused_computation.5 | convolution fusion | flops 264241152 | bytes 2818048 | tf_op jit(solution)/shard_map/dot_general | solution.py:606
  12.2 0.0 all-gather.9.cloned.1.call-start
  12.3 1.7 copy-done.22
  13.9 4.1 %pick_pages.1 = (s32[2]{0:T(128)S(1)}, bf16[8,16,1152]{2,1,0:T(8,128)(2,1)}, bf16[8,16,1152]{2,1,0:T(8,128)(2,1)S(1)}, bf16[1,16,16,1152]{3,2,1,0:T(8,128)(2,1)S(1)}) custom-call(s32[2,64]{1,0:T(2,128)S(1)} %bitcast.34, s32[2,64]{1,0:T(2,128)S(1)} %copy-done.24, bf16[32,36864]{1,0:T(8,128)(2,1)S(1)} %copy-done.22), custom_call_target="tpu_custom_call" | custom-call | flops 1000000000 | bytes 6000000 | tf_op jit(solution)/shard_map/pick_pages/pallas_call | solution.py:143
  18.1 0.0 all-gather.11.cloned.1.call-start
  18.2 3.0 %collective-permute-start = (bf16[16,16,1152]{2,1,0:T(8,128)(2,1)S(1)}, bf16[16,16,1152]{2,1,0:T(8,128)(2,1)S(1)}, u32[]{:S(2)}, u32[]{:S(2)}) collective-permute-start(bf16[16,16,1152]{2,1,0:T(8,128)(2,1)S(1)} %bitcast.36), channel_id=1, source_target_pairs={{0,2},{2,0},{1,3},{3,1},{4,6},{6,4},{5,7},{7,5},{8,10},{10,8},{9,1... | collective-permute-start | bytes 1769480 | tf_op jit(solution)/shard_map/ppermute | solution.py:590
  21.2 13.3 %collective-permute-done.refs_0_ = bf16[16,16,1152]{2,1,0:T(8,128)(2,1)S(1)} collective-permute-done((bf16[16,16,1152]{2,1,0:T(8,128)(2,1)S(1)}, bf16[16,16,1152]{2,1,0:T(8,128)(2,1)S(1)}, u32[]{:S(2)}, u32[]{:S(2)}) %collective-permute-start) | collective-permute-done | bytes 589856 | tf_op jit(solution)/shard_map/ppermute | solution.py:590
  34.5 2.9 %join_pages.1 = (bf16[8,16,1152]{2,1,0:T(8,128)(2,1)}, bf16[8,16,1152]{2,1,0:T(8,128)(2,1)}, bf16[8,16,1152]{2,1,0:T(8,128)(2,1)S(1)}) custom-call(s32[2]{0:T(128)S(1)} %get-tuple-element.30.count_ref, bf16[8,16,1152]{2,1,0:T(8,128)(2,1)S(1)} %get-tuple-element.31.rest_ref, bf16[16,16,1152]{2,1,0:T(8,128)(2,1)S(1)} %collective-permute-done.refs_0_), custom_call_target="tpu_custom_call" | custom-call | bytes 3000000 | tf_op jit(solution)/shard_map/join_pages/pallas_call | solution.py:196
  37.5 0.7 copy-done.20
  38.2 0.0 all-gather.13.cloned.1.call-start
  38.2 0.5 all-gather.13.cloned.1.call-update
  38.8 0.2 copy.30
  39.1 0.2 copy.37
  39.3 0.6 dynamic_slice.12
  39.9 0.6 dynamic_slice.13.suffix_ref
  40.5 0.6 add_compare_fusion
  41.1 0.1 broadcast_in_dim.58
  41.2 0.9 broadcast_in_dim.59
  42.1 0.7 subtract_clamp_fusion
  42.9 0.7 add_convert_fusion.1
  43.6 1.1 fusion.4
  44.8 0.2 convert_reduce_fusion
  45.0 0.1 select_reduce_fusion.limit_ref
  45.1 0.3 multiply_cosine_fusion
  45.4 0.3 subtract_convert_fusion
  45.7 0.5 convolution_convert_fusion
  46.2 0.2 pad_maximum_fusion
  46.4 0.1 fusion.5
  46.5 13.2 %all-reduce.2.cloned.1.call-done = f32[128,576]{1,0:T(8,128)} async-done(((f32[128,576]{1,0:T(8,128)}), f32[128,576]{1,0:T(8,128)}) %all-reduce.2.cloned.1.call-update) | async-done | bytes 294928 | tf_op jit(solution)/shard_map/psum | solution.py:607
  59.7 1.1 multiply_reduce_fusion
  60.7 1.2 multiply_subtract_fusion
  62.0 1.0 multiply_multiply_fusion
  63.0 1.4 broadcast_select_fusion
  64.5 1.9 %collective-permute-start.1 = (bf16[128,576]{1,0:T(8,128)(2,1)S(1)}, bf16[128,576]{1,0:T(8,128)(2,1)}, u32[]{:S(2)}, u32[]{:S(2)}) collective-permute-start(bf16[128,576]{1,0:T(8,128)(2,1)S(1)} %get-tuple-element.48.fresh_ref), channel_id=1, source_target_pairs={{0,1},{2,3},{4,5},{6,7},{8,9},{10,11},{12,13},{14,15},{16,17},{18,... | collective-permute-start | bytes 442376 | tf_op jit(solution)/shard_map/ppermute | solution.py:18
  66.4 1.8 convert_element_type.44
  68.2 1.9 %broadcast_select_fusion.1 = bf16[1,2,36864]{2,1,0:T(2,128)(2,1)} fusion(pred[1,2,36864]{2,1,0:T(4,128)(4,1)} %broadcast_in_dim.59, bf16[1,2,36864]{2,1,0:T(2,128)(2,1)} %convert_element_type.44), kind=kLoop, calls=%fused_computation.14 | loop fusion | flops 73728 | bytes 368640 | tf_op jit(solution)/shard_map/jit(_where)/select_n | solution.py:48
  70.1 1.7 copy-done.23
  71.8 8.9 %score_part.3 = (f32[12,1024,512]{2,1,0:T(8,128)}, bf16[12,512,512]{2,1,0:T(8,128)(2,1)}, f32[1024,12]{1,0:T(8,128)S(1)}, f32[1024,1]{1,0:T(8,128)S(1)}, f32[1024,1]{1,0:T(8,128)S(1)}) custom-call(s32[32]{0:T(128)S(1)} %get-tuple-element.59.limit_ref, bf16[1024,576]{1,0:T(8,128)(2,1)S(1)} %bitcast.30, bf16[4,2,8,16,1152]{4,3,2,1,0:T(8,128)(2,1)S(1)} %bitcast.35), custom_call_target="tpu_custom_call" | custom-call | flops 2415919104 | bytes 10000000 | tf_op jit(solution)/shard_map/score_part/pallas_call | solution.py:357
  80.7 0.8 copy-done.14
  81.5 0.8 copy-done.16
  82.3 0.8 copy-done.18
  83.1 2.1 %all-gather.11.cloned.1.call-done = bf16[64,16,1152]{2,1,0:T(8,128)(2,1)} async-done(((bf16[8,16,1152]{2,1,0:T(8,128)(2,1)}), bf16[64,16,1152]{2,1,0:T(8,128)(2,1)}) %all-gather.11.cloned.1.call-update) | async-done | bytes 2359312 | tf_op jit(solution)/shard_map/all_gather | solution.py:594
  85.2 1.0 copy-done.15
  86.2 1.0 copy-done.17
  87.3 1.0 copy-done.19
  88.3 9.3 %score_part.4 = (f32[12,1024,512]{2,1,0:T(8,128)}, bf16[12,512,512]{2,1,0:T(8,128)(2,1)}, f32[1024,12]{1,0:T(8,128)S(1)}, f32[1024,1]{1,0:T(8,128)S(1)}, f32[1024,1]{1,0:T(8,128)S(1)}) custom-call(s32[32]{0:T(128)S(1)} %get-tuple-element.60.limit_ref, bf16[1024,576]{1,0:T(8,128)(2,1)S(1)} %bitcast.31, ...), custom_call_target="tpu_custom_call", output_to_operand_aliasing={{0}: (5, {}), {1}: (6, {})} | custom-call | flops 2415919104 | bytes 10000000 | tf_op jit(solution)/shard_map/score_part/pallas_call | solution.py:357
  97.6 0.8 copy-done.8
  98.4 0.8 copy-done.10
  99.2 0.8 copy-done.12
  100.0 17.3 %all-gather.13.cloned.1.call-done = bf16[64,16,1152]{2,1,0:T(8,128)(2,1)} async-done(((bf16[8,16,1152]{2,1,0:T(8,128)(2,1)}), bf16[64,16,1152]{2,1,0:T(8,128)(2,1)}) %all-gather.13.cloned.1.call-update) | async-done | bytes 2359312 | tf_op jit(solution)/shard_map/all_gather | solution.py:594
  117.4 1.0 copy-done.9
  118.4 1.0 copy-done.11
  119.4 1.0 copy-done.13
  120.5 6.6 %score_part.5 = (f32[12,1024,512]{2,1,0:T(8,128)}, bf16[12,512,512]{2,1,0:T(8,128)(2,1)}, f32[1024,12]{1,0:T(8,128)S(1)}, f32[1024,1]{1,0:T(8,128)S(1)}, f32[1024,1]{1,0:T(8,128)S(1)}) custom-call(s32[32]{0:T(128)S(1)} %get-tuple-element.61.limit_ref, bf16[1024,576]{1,0:T(8,128)(2,1)S(1)} %bitcast.32, ...), custom_call_target="tpu_custom_call", output_to_operand_aliasing={{0}: (5, {}), {1}: (6, {})} | custom-call | flops 2415919104 | bytes 10000000 | tf_op jit(solution)/shard_map/score_part/pallas_call | solution.py:357
  127.1 0.8 copy-done.2
  127.9 0.8 copy-done.4
  128.7 0.8 copy-done.6
  129.5 20.1 %all-gather.15.cloned.1.call-done = bf16[64,16,1152]{2,1,0:T(8,128)(2,1)} async-done(((bf16[8,16,1152]{2,1,0:T(8,128)(2,1)}), bf16[64,16,1152]{2,1,0:T(8,128)(2,1)}) %all-gather.15.cloned.1.call-update) | async-done | bytes 2359312 | tf_op jit(solution)/shard_map/all_gather | solution.py:594
  149.6 1.2 copy-done.1
  150.9 1.0 copy-done.3
  151.9 1.0 copy-done.5
  152.9 1.0 copy-done.7
  154.0 22.8 %finish.1 = bf16[128,1024]{1,0:T(8,128)(2,1)} custom-call(s32[128]{0:T(128)S(1)} %select_reduce_fusion.limit_ref, bf16[1024,576]{1,0:T(8,128)(2,1)S(1)} %bitcast.33, f32[1024,12]{1,0:T(8,128)S(1)} %copy-done.3, f32[1024,1]{1,0:T(8,128)S(1)} %copy-done.5, f32[1024,1]{1,0:T(8,128)S(1)} %copy-done.7, f32[12,1024,512]{2,1,0:T(8,128)} %get-tuple-element.43.weights_hbm, ...), custom_call_target="tpu_custom_call" | custom-call | flops 8589934592 | bytes 30000000 | tf_op jit(solution)/shard_map/finish/pallas_call | solution.py:518
  (53 shorter events, 0.4 us)
Async XLA Ops:
  8.0 1.6 copy-start
  8.0 4.2 %copy-start.21 = (s32[2,64,1]{1,2,0:T(1,128)S(1)}, s32[2,64,1]{1,2,0:T(1,128)}, u32[]{:S(2)}) copy-start(s32[2,64,1]{1,2,0:T(1,128)} %param.18) | copy-start | bytes 1540
  8.0 4.2 %copy-start.24 = (s32[2,64]{1,0:T(2,128)S(1)}, s32[2,64]{1,0:T(2,128)}, u32[]{:S(2)}) copy-start(s32[2,64]{1,0:T(2,128)} %slot_hbm.1) | copy-start | bytes 1540
  8.0 51.6 %all-reduce.2.cloned.1.call-start = ((), (), s32[]{:S(2)}) async-start(), calls=%async_computation | async-start | bytes 655360 | tf_op jit(solution)/shard_map/psum | solution.py:607
  12.2 57.9 %all-gather.9.cloned.1.call-start = ((), (), s32[]{:S(2)}) async-start(), calls=%async_computation.1 | async-start | bytes 2654208 | tf_op jit(solution)/shard_map/all_gather | solution.py:588
  12.3 1.7 copy-start.22
  13.9 24.9 %copy-start.26 = (bf16[1,128,1536]{2,1,0:T(8,128)(2,1)S(1)}, bf16[1,128,1536]{2,1,0:T(8,128)(2,1)}, u32[]{:S(2)}) copy-start(bf16[1,128,1536]{2,1,0:T(8,128)(2,1)} %param.11) | copy-start | bytes 1179652
  18.1 21.2 %copy-start.28 = (s32[2]{0:T(128)S(1)}, s32[2]{0:T(128)}, u32[]{:S(2)}) copy-start(s32[2]{0:T(128)} %param.20) | copy-start | bytes 28
  18.1 21.8 %copy-start.29 = (s32[2]{0:T(128)S(1)}, s32[2]{0:T(128)}, u32[]{:S(2)}) copy-start(s32[2]{0:T(128)} %param.21) | copy-start | bytes 28
  18.1 67.1 %all-gather.11.cloned.1.call-start = ((), (), s32[]{:S(2)}) async-start(), calls=%async_computation.2 | async-start | bytes 2654208 | tf_op jit(solution)/shard_map/all_gather | solution.py:594
  18.2 16.3 %collective-permute-start = (bf16[16,16,1152]{2,1,0:T(8,128)(2,1)S(1)}, bf16[16,16,1152]{2,1,0:T(8,128)(2,1)S(1)}, u32[]{:S(2)}, u32[]{:S(2)}) collective-permute-start(bf16[16,16,1152]{2,1,0:T(8,128)(2,1)S(1)} %bitcast.36), channel_id=1, source_target_pairs={{0,2},{2,0},{1,3},{3,1},{4,6},{6,4},{5,7},{7,5},{8,10},{10,8},{9,1... | collective-permute-start | bytes 1769480 | tf_op jit(solution)/shard_map/ppermute | solution.py:590
  37.5 0.7 copy-start.20
  38.2 79.2 %all-gather.13.cloned.1.call-start = ((), (), s32[]{:S(2)}) async-start(), calls=%async_computation.3 | async-start | bytes 2654208 | tf_op jit(solution)/shard_map/all_gather | solution.py:594
  38.8 110.9 %all-gather.15.cloned.1.call-start = ((), (), s32[]{:S(2)}) async-start(), calls=%async_computation.4 | async-start | bytes 2654208 | tf_op jit(solution)/shard_map/all_gather | solution.py:594
  42.1 3.6 %copy-start.25 = (bf16[8,128,512]{2,1,0:T(8,128)(2,1)S(1)}, bf16[8,128,512]{2,1,0:T(8,128)(2,1)}, u32[]{:S(2)}) copy-start(bf16[8,128,512]{2,1,0:T(8,128)(2,1)} %param.15) | copy-start | bytes 3145732
  45.7 16.3 %copy-start.27 = (f32[512]{0:T(512)S(1)}, f32[512]{0:T(512)}, u32[]{:S(2)}) copy-start(f32[512]{0:T(512)} %param.14) | copy-start | bytes 6148
  64.5 65.1 %collective-permute-start.1 = (bf16[128,576]{1,0:T(8,128)(2,1)S(1)}, bf16[128,576]{1,0:T(8,128)(2,1)}, u32[]{:S(2)}, u32[]{:S(2)}) collective-permute-start(bf16[128,576]{1,0:T(8,128)(2,1)S(1)} %get-tuple-element.48.fresh_ref), channel_id=1, source_target_pairs={{0,1},{2,3},{4,5},{6,7},{8,9},{10,11},{12,13},{14,15},{16,17},{18,... | collective-permute-start | bytes 442376 | tf_op jit(solution)/shard_map/ppermute | solution.py:18
  70.1 1.7 copy-start.23
  80.7 0.8 copy-start.14
  81.5 0.8 copy-start.16
  82.3 0.8 copy-start.18
  85.2 1.0 copy-start.15
  86.2 1.0 copy-start.17
  87.3 1.0 copy-start.19
  97.6 0.8 copy-start.8
  98.4 0.8 copy-start.10
  99.2 0.8 copy-start.12
  117.4 1.0 copy-start.9
  118.4 1.0 copy-start.11
  119.4 1.0 copy-start.13
  127.1 0.8 copy-start.2
  127.9 0.8 copy-start.4
  128.7 0.8 copy-start.6
  149.6 1.2 copy-start.1
  150.8 1.0 copy-start.3
  151.9 1.0 copy-start.5
  152.9 1.0 copy-start.7
Sparse Core Ops, SparseCore 0:
  12.3 47.3 all-reduce.1
Sparse Core Ops, SparseCore 1:
  18.2 34.7 all-gather.8
  54.4 30.7 all-gather.10
  86.7 30.6 all-gather.12
  119.0 30.6 all-gather.14
